TPU v7x, 32 devices: a whole 2x2x4 slice. The times are simulated.
32 devices in a mesh: groups: 2 (over y), block: 4 (over z), rep: 2 (over x), tile: 2 (over core).
Axes of the slice: x: 2, y: 2, z: 4, core: 2. Of those that a mesh axis runs over, the one named last changes fastest.
Arguments:
- visible: int32 [8, 512, 2], P(('groups', 'block'), ('rep', 'tile')), parts along dimension 0, may hold values from 0 to 11, all different within a row; in each aligned block of 128 rows (0 to 127, 128 to 255, ..., all dimensions but the last counted through in order) at most 43 rows name the same one
- bins: int32 [8, 512, 2, 16], P(('groups', 'block'), ('rep', 'tile')), parts along dimension 0, may hold values from 0 to 255, as said below
- ray_code: bfloat16 [8, 512, 128], P(('groups', 'block'), ('rep', 'tile')), parts along dimension 0, may hold values from -6 to 6
- blend: float32 [8, 512, 2], P(('groups', 'block'), ('rep', 'tile')), parts along dimension 0, may hold values from 0.2 to 5
- truth: float32 [3, 8, 512], P(None, ('groups', 'block'), ('rep', 'tile')), parts along dimension 1, may hold values from 0 to 1
- w_in: bfloat16 [12, 144, 512], P('block'), may hold values from -0.75 to 0.75
- w_hid: bfloat16 [12, 512, 512], P('block'), may hold values from -0.375 to 0.375
- w_out: bfloat16 [12, 4, 512], P('block'), may hold values from -0.5 to 0.5
Outputs:
- rendered: float32 [3, 8, 512], P(None, ('groups', 'block'), ('rep', 'tile')), parts along dimension 1
- flip_map: float32 [8, 512], P(('groups', 'block'), ('rep', 'tile')), parts along dimension 0
- psnr: float32 [2], P('groups'), parts along dimension 0
There are 2 independent parts, one for each index of `groups`. A program takes and returns all parts, laid end to end along the dimension named above; an argument that names none is the same for every part. Nothing has to cross between parts.
Inputs may be any that keep to these rules, and one draw needn't show every extreme that they name: `visible`: each pixel names 2 different blocks; among the 128 pixels of one device no block is named by more than 43 pixels, and some block is named by exactly 43. `bins`: sample j of every list lies in [j * 16, (j + 1) * 16), so each list rises.
All inputs are finite; a program needn't handle non-finite values.
Results may differ from a plain program's by a relative error of at most 0.00061.
Values may be sent and summed in bfloat16 or wider, within the bound.
No kernel may reach another device: no remote copies, remote signals or barrier semaphores. Data moves between devices by JAX's collectives and lax.ppermute only.
A program may use at most 64 MiB of HBM per device.

v0:
```python
import jax
import jax.numpy as jnp
from jax import lax
from jax.sharding import PartitionSpec as P

RC = 128
DC = 16
NBINS = 256


OPPONENT = ((0.2126, 0.7152, 0.0722), (0.5, -0.5, 0.0), (0.0, 0.4, -0.4))
SPREAD = (0.6, 0.35, 0.35)
EMPHASIS = (1.0, 2.0, 2.0)


def extended(block, sides, width):
    for axis, dim in sides:
        count = lax.axis_size(axis)
        forward = [(i, i + 1) for i in range(count - 1)]
        backward = [(target, source) for source, target in forward]
        low = lax.ppermute(
            lax.slice_in_dim(block, block.shape[dim] - width, None, axis=dim), axis, forward
        )
        high = lax.ppermute(lax.slice_in_dim(block, 0, width, axis=dim), axis, backward)
        block = jnp.concatenate([low, block, high], axis=dim)
    return block


def make_inputs(ray_codes, depth_bins):
    pair_num = depth_bins.shape[0]
    sample_num = depth_bins.shape[1]
    powers = jnp.arange(DC // 2, dtype=jnp.float32)
    angles = depth_bins[:, :, None] * (jnp.pi * jnp.exp2(powers) / NBINS)
    depth_code = jnp.concatenate([jnp.sin(angles), jnp.cos(angles)], axis=2).astype(jnp.bfloat16)
    spread_codes = jnp.broadcast_to(
        ray_codes[:, None, :], (pair_num, sample_num, ray_codes.shape[1])
    )
    return jnp.concatenate([spread_codes, depth_code], axis=2)


def network(inputs, weight_in, weight_hidden, weight_out):
    pair_num = inputs.shape[0]
    sample_num = inputs.shape[1]
    flattened = inputs.reshape(pair_num * sample_num, inputs.shape[2])
    layer_one = jnp.maximum(
        jnp.dot(flattened, weight_in, preferred_element_type=jnp.float32), 0.0
    ).astype(jnp.bfloat16)
    layer_two = jnp.maximum(
        jnp.dot(layer_one, weight_hidden, preferred_element_type=jnp.float32), 0.0
    ).astype(jnp.bfloat16)
    outputs = lax.dot_general(
        weight_out, layer_two, (((1,), (1,)), ((), ())), preferred_element_type=jnp.float32
    )
    return outputs.reshape(4, pair_num, sample_num)


def composite(outputs):
    sample_num = outputs.shape[2]
    optical = jax.nn.softplus(outputs[0]) * (1.5 / sample_num)
    before = jnp.cumsum(optical, axis=1) - optical
    weights = jnp.exp(-before) * (1.0 - jnp.exp(-optical))
    colors = jnp.sum(weights[None] * jax.nn.sigmoid(outputs[1:]), axis=2)
    return jnp.concatenate([colors, jnp.sum(weights, axis=1)[None]], axis=0)


def opponent_error(rendered, truth):
    matrix = jnp.array(OPPONENT, dtype=jnp.float32)
    return jnp.einsum("ij,jhw->ihw", matrix, rendered - truth, precision=lax.Precision.HIGHEST)


def flip_from(padded):
    neighbour = jnp.array(SPREAD, dtype=jnp.float32)[:, None, None]
    emphasis = jnp.array(EMPHASIS, dtype=jnp.float32)[:, None, None]
    rowwise = neighbour * padded[:, :-2, :] + padded[:, 1:-1, :] + neighbour * padded[:, 2:, :]
    colwise = neighbour * rowwise[:, :, :-2] + rowwise[:, :, 1:-1] + neighbour * rowwise[:, :, 2:]
    filtered = colwise / ((1.0 + 2.0 * neighbour) * (1.0 + 2.0 * neighbour))
    return jnp.sqrt(jnp.sum((emphasis * filtered) ** 2, axis=0) + 1e-06)


def arrange(served, sources, count_slots):
    trailing = served.shape[3:]
    regrouped = served.reshape((served.shape[0], 4, sources, count_slots) + trailing)
    return jnp.transpose(regrouped, (2, 0, 3, 1) + tuple(range(4, regrouped.ndim)))


def body(visible, bins, ray_code, blend, truth, w_in, w_hid, w_out):
    block_count = lax.axis_size("block")
    column_devices = lax.axis_size("rep") * lax.axis_size("tile")
    local_blocks = w_in.shape[0]
    in_width = w_in.shape[1]
    pixels = visible.shape[1]
    visible_num = visible.shape[2]
    sample_num = bins.shape[3]
    pair_count = pixels * visible_num
    blocks_all = local_blocks * block_count
    capacity = (2 * pair_count + blocks_all - 1) // blocks_all
    slot_total = blocks_all * capacity
    block_of = visible.reshape(pair_count)
    position = jnp.arange(pair_count, dtype=jnp.int32)
    earlier = (block_of[None, :] == block_of[:, None]) & (position[None, :] < position[:, None])
    slot_of = block_of * capacity + jnp.sum(earlier.astype(jnp.int32), axis=1)
    depth_bins = bins.reshape(pair_count, sample_num)
    ray_codes = jnp.repeat(ray_code.reshape(pixels, RC), visible_num, axis=0)
    encoded = make_inputs(ray_codes, depth_bins.astype(jnp.float32)).reshape(
        pair_count, sample_num * in_width
    )
    encoded_slots = (
        jnp.zeros((slot_total, sample_num * in_width), jnp.bfloat16).at[slot_of].set(encoded)
    )
    received = lax.all_to_all(
        encoded_slots.reshape(block_count, local_blocks, capacity, sample_num * in_width),
        "block",
        split_axis=0,
        concat_axis=0,
        tiled=True,
    )
    sources = received.shape[0]
    count_slots = received.shape[2]
    input_rows = jnp.transpose(received, (1, 0, 2, 3)).reshape(
        local_blocks, sources * count_slots, sample_num, in_width
    )

    def per_block_encoded(operands):
        inputs_here, weight_in, weight_hidden, weight_out = operands
        return network(inputs_here, weight_in, weight_hidden, weight_out)

    served = arrange(
        lax.map(per_block_encoded, (input_rows, w_in, w_hid, w_out)), sources, count_slots
    )
    flattened = served.reshape(block_count, -1)
    came_back = lax.all_to_all(
        flattened.astype(jnp.bfloat16), "block", split_axis=0, concat_axis=0, tiled=True
    ).astype(flattened.dtype)
    per_sample = came_back.reshape(slot_total, 4, sample_num)[slot_of]
    pair_colors = composite(jnp.transpose(per_sample, (1, 0, 2))).T
    pieces = pair_colors.reshape(pixels, visible_num, 4)
    with_background = pieces[:, :, :3] + (1.0 - pieces[:, :, 3:])
    weights = blend.reshape(pixels, visible_num)[:, :, None]
    rendered = (jnp.sum(weights * with_background, axis=1) / jnp.sum(weights, axis=1)).T.reshape(
        3, 1, pixels
    )
    difference = rendered - truth
    squared = lax.psum(jnp.sum(difference * difference), ("block", "rep", "tile"))
    mean_square = squared / (3 * block_count * column_devices * pixels)
    psnr = (-10.0 * jnp.log10(mean_square + 1e-06)).reshape(1)
    padded = extended(opponent_error(rendered, truth), (("block", 1), (("rep", "tile"), 2)), 1)
    flip_map = flip_from(padded)
    return (rendered, flip_map, psnr)


def solution(mesh):
    placed = (
        P(("groups", "block"), ("rep", "tile"), None),
        P(("groups", "block"), ("rep", "tile"), None, None),
        P(("groups", "block"), ("rep", "tile"), None),
        P(("groups", "block"), ("rep", "tile"), None),
        P(None, ("groups", "block"), ("rep", "tile")),
        P("block", None, None),
        P("block", None, None),
        P("block", None, None),
    )
    return jax.shard_map(
        body,
        mesh=mesh,
        in_specs=placed,
        out_specs=(
            P(None, ("groups", "block"), ("rep", "tile")),
            P(("groups", "block"), ("rep", "tile")),
            P("groups"),
        ),
        check_vma=False,
    )
```

profile of v0, /device:TPU:0, one launch (start us, length us, event | category | flops | bytes accessed | tf_op | source)
XLA Modules:
  0.0 175.7 jit_solution(7349004769962199136)
XLA Ops:
  0.6 0.8 copy.76
  1.4 0.7 broadcast_multiply_fusion
  2.1 0.7 convert_element_type.47
  3.0 0.8 broadcast_in_dim.16
  3.9 0.5 fusion.23
  4.7 1.5 copy.80
  6.3 0.2 convert_reduce_fusion
  6.6 0.1 mul.121
  6.8 3.8 %scatter_custom_fusion = bf16[516,2304]{1,0:T(8,128)(2,1)S(1)} fusion(s32[256]{0:T(256)S(1)} %bitcast.109, bf16[256,2304]{1,0:T(8,128)(2,1)} %copy.80, bf16[]{:T(256)} %constant.26.clone.1), kind=kCustom, calls=%fused_computation.18 | custom fusion | bytes 2378240 | tf_op jit(solution)/shard_map/scatter | solution.py:108
  10.6 2.0 %reshape.146 = bf16[4,3,43,2304]{3,2,1,0:T(8,128)(2,1)} reshape(bf16[516,2304]{1,0:T(8,128)(2,1)S(1)} %scatter_custom_fusion) | data formatting | bytes 4755456 | tf_op jit(solution)/shard_map/reshape | solution.py:111
  12.7 6.4 %all-to-all-start = ((bf16[4,3,43,2304]{3,2,1,0:T(8,128)(2,1)}), bf16[4,3,43,2304]{3,2,1,0:T(8,128)(2,1)S(1)}, u32[]{:S(2)}, u32[]{:S(2)}) async-start(bf16[4,3,43,2304]{3,2,1,0:T(8,128)(2,1)} %reshape.146), calls=%async_computation | async-start | bytes 5308416 | tf_op jit(solution)/shard_map/all_to_all | solution.py:110
  19.4 59.9 %all-to-all-done = bf16[4,3,43,2304]{3,2,1,0:T(8,128)(2,1)S(1)} async-done(((bf16[4,3,43,2304]{3,2,1,0:T(8,128)(2,1)}), bf16[4,3,43,2304]{3,2,1,0:T(8,128)(2,1)S(1)}, u32[]{:S(2)}, u32[]{:S(2)}) %all-to-all-start) | async-done | bytes 2377760 | tf_op jit(solution)/shard_map/all_to_all | solution.py:110
  79.2 1.7 copy.81
  81.0 9.3 %reshape.147 = bf16[3,172,16,144]{3,2,1,0:T(8,128)(2,1)} reshape(bf16[3,4,43,2304]{3,2,1,0:T(8,128)(2,1)} %copy.81) | data formatting | bytes 4755456 | tf_op jit(solution)/shard_map/reshape | solution.py:119
  90.2 26.2 %while.10 = (s32[]{:T(128)}, bf16[3,4,172,16]{2,1,3,0:T(4,128)(2,1)S(1)}, bf16[3,4,512]{2,1,0:T(4,128)(2,1)}, bf16[3,172,16,144]{3,2,1,0:T(8,128)(2,1)}, bf16[3,...) while((s32[]{:T(128)}, bf16[3,4,172,16]{2,1,3,0:T(4,128)(2,1)S(1)}, ...), condition=%wide.region_3.4_spmd, body=%wide.region_2.3_spmd.sunk | while | flops 1865547776 | bytes 9373777 | solution.py:128
  90.2 2.5 %constant_dynamic-slice_fusion.2 = bf16[1,172,16,144]{3,2,1,0:T(8,128)(2,1)} fusion(bf16[3,172,16,144]{3,2,1,0:T(8,128)(2,1)} %get-tuple-element.117, s32[]{:T(128)} %get-tuple-element.107), kind=kLoop, calls=%fused_computation.15.clone.1 | loop fusion | bytes 1585156 | tf_op jit(solution)/shard_map/while/body/jit(dynamic_index_in_dim)/dynamic_slice | solution.py:128
  92.8 3.9 %maximum_convert_fusion.3 = bf16[2752,512]{1,0:T(8,128)(2,1)S(1)} fusion(bf16[2752,144]{1,0:T(8,128)(2,1)} %bitcast.95, bf16[3,512,512]{2,1,0:T(8,128)(2,1)} %get-tuple-element.119, s32[]{:T(128)} %get-tuple-element.107, bf16[3,144,512]{2,1,0:T(8,128)(2,1)} %get-tuple-element.118), kind=kOutput, calls=%fused_computation.2.clone.1 | convolution fusion | flops 1854275584 | bytes 4899840 | tf_op jit(solution)/shard_map/while/body/eval_jaxpr/dot_general | solution.py:49
  96.6 2.3 %fusion.64 = bf16[3,4,172,16]{2,1,3,0:T(4,128)(2,1)S(1)} fusion(bf16[3,4,172,16]{2,1,3,0:T(4,128)(2,1)S(1)} %get-tuple-element.108, s32[]{:T(128)} %get-tuple-element.107, bf16[172,16,512]{2,1,0:T(8,128)(2,1)S(1)} %bitcast.94, bf16[3,4,512]{2,1,0:T(4,128)(2,1)} %get-tuple-element.116), kind=kOutput, calls=%fused_computation.7.clone.1 | convolution fusion | flops 11272192 | bytes 2888704 | tf_op jit(solution)/shard_map/while/body/eval_jaxpr/dot_general | solution.py:51
  98.9 2.5 %constant_dynamic-slice_fusion.2 = bf16[1,172,16,144]{3,2,1,0:T(8,128)(2,1)} fusion(bf16[3,172,16,144]{3,2,1,0:T(8,128)(2,1)} %get-tuple-element.117, s32[]{:T(128)} %get-tuple-element.107), kind=kLoop, calls=%fused_computation.15.clone.1 | loop fusion | bytes 1585156 | tf_op jit(solution)/shard_map/while/body/jit(dynamic_index_in_dim)/dynamic_slice | solution.py:128
  101.5 3.9 %maximum_convert_fusion.3 = bf16[2752,512]{1,0:T(8,128)(2,1)S(1)} fusion(bf16[2752,144]{1,0:T(8,128)(2,1)} %bitcast.95, bf16[3,512,512]{2,1,0:T(8,128)(2,1)} %get-tuple-element.119, s32[]{:T(128)} %get-tuple-element.107, bf16[3,144,512]{2,1,0:T(8,128)(2,1)} %get-tuple-element.118), kind=kOutput, calls=%fused_computation.2.clone.1 | convolution fusion | flops 1854275584 | bytes 4899840 | tf_op jit(solution)/shard_map/while/body/eval_jaxpr/dot_general | solution.py:49
  105.4 2.3 %fusion.64 = bf16[3,4,172,16]{2,1,3,0:T(4,128)(2,1)S(1)} fusion(bf16[3,4,172,16]{2,1,3,0:T(4,128)(2,1)S(1)} %get-tuple-element.108, s32[]{:T(128)} %get-tuple-element.107, bf16[172,16,512]{2,1,0:T(8,128)(2,1)S(1)} %bitcast.94, bf16[3,4,512]{2,1,0:T(4,128)(2,1)} %get-tuple-element.116), kind=kOutput, calls=%fused_computation.7.clone.1 | convolution fusion | flops 11272192 | bytes 2888704 | tf_op jit(solution)/shard_map/while/body/eval_jaxpr/dot_general | solution.py:51
  107.7 2.5 %constant_dynamic-slice_fusion.2 = bf16[1,172,16,144]{3,2,1,0:T(8,128)(2,1)} fusion(bf16[3,172,16,144]{3,2,1,0:T(8,128)(2,1)} %get-tuple-element.117, s32[]{:T(128)} %get-tuple-element.107), kind=kLoop, calls=%fused_computation.15.clone.1 | loop fusion | bytes 1585156 | tf_op jit(solution)/shard_map/while/body/jit(dynamic_index_in_dim)/dynamic_slice | solution.py:128
  110.2 3.9 %maximum_convert_fusion.3 = bf16[2752,512]{1,0:T(8,128)(2,1)S(1)} fusion(bf16[2752,144]{1,0:T(8,128)(2,1)} %bitcast.95, bf16[3,512,512]{2,1,0:T(8,128)(2,1)} %get-tuple-element.119, s32[]{:T(128)} %get-tuple-element.107, bf16[3,144,512]{2,1,0:T(8,128)(2,1)} %get-tuple-element.118), kind=kOutput, calls=%fused_computation.2.clone.1 | convolution fusion | flops 1854275584 | bytes 4899840 | tf_op jit(solution)/shard_map/while/body/eval_jaxpr/dot_general | solution.py:49
  114.1 2.3 %fusion.64 = bf16[3,4,172,16]{2,1,3,0:T(4,128)(2,1)S(1)} fusion(bf16[3,4,172,16]{2,1,3,0:T(4,128)(2,1)S(1)} %get-tuple-element.108, s32[]{:T(128)} %get-tuple-element.107, bf16[172,16,512]{2,1,0:T(8,128)(2,1)S(1)} %bitcast.94, bf16[3,4,512]{2,1,0:T(4,128)(2,1)} %get-tuple-element.116), kind=kOutput, calls=%fused_computation.7.clone.1 | convolution fusion | flops 11272192 | bytes 2888704 | tf_op jit(solution)/shard_map/while/body/eval_jaxpr/dot_general | solution.py:51
  116.4 0.1 convert_element_type.50
  116.6 0.4 copy.82
  117.0 0.4 convert_element_type.56
  117.4 0.5 broadcast.104
  117.9 1.0 reduce.5
  118.9 0.7 reshape.173
  119.7 3.5 %all-to-all-start.1 = ((bf16[4,2,4128]{2,1,0:T(2,128)(2,1)}), bf16[4,2,4128]{2,1,0:T(2,128)(2,1)S(1)}, u32[]{:S(2)}, u32[]{:S(2)}) async-start(bf16[4,2,4128]{2,1,0:T(2,128)(2,1)} %reshape.173), calls=%async_computation.1 | async-start | bytes 135168 | tf_op jit(solution)/shard_map/all_to_all | solution.py:131
  123.2 5.5 %all-to-all-done.1 = bf16[4,2,4128]{2,1,0:T(2,128)(2,1)S(1)} async-done(((bf16[4,2,4128]{2,1,0:T(2,128)(2,1)}), bf16[4,2,4128]{2,1,0:T(2,128)(2,1)S(1)}, u32[]{:S(2)}, u32[]{:S(2)}) %all-to-all-start.1) | async-done | bytes 66080 | tf_op jit(solution)/shard_map/all_to_all | solution.py:131
  128.8 0.4 convert_reduce_fusion.1
  129.2 0.5 reshape.152
  129.8 1.0 gather_fusion
  130.8 0.2 copy.84
  131.3 0.2 slice.53
  131.7 0.4 fusion.26
  132.1 0.7 multiply_reduce_fusion
  132.8 0.2 convolution_bitcast_fusion
  133.0 2.9 %collective-permute-start = (f32[3,1,128]{2,0,1:T(4,128)S(1)}, f32[3,1,128]{2,0,1:T(4,128)S(1)}, u32[]{:S(2)}, u32[]{:S(2)}) collective-permute-start(f32[3,1,128]{2,0,1:T(4,128)S(1)} %convolution_bitcast_fusion), channel_id=1, source_target_pairs={{0,4},{4,8},{8,12},{1,5},{5,9},{9,13},{2,6},{6,10},{10,14},{3,7},{... | collective-permute-start | bytes 4616 | tf_op jit(solution)/shard_map/ppermute | solution.py:21
  135.8 1.3 collective-permute-start.1
  137.1 30.8 %psum.7 = f32[]{:T(128)} all-reduce(f32[]{:T(128)} %get-tuple-element.57), channel_id=1, replica_groups=mesh['groups'=2,'block'=4,'rep'=2,'tile'=2] {'block','rep','tile'}, use_global_device_ids=true, to_apply=%region_11.12 | all-reduce | flops 1 | bytes 8 | tf_op jit(solution)/shard_map/psum | solution.py:143
  167.9 0.6 copy.89
  169.4 1.3 collective-permute-start.2
  170.7 1.3 collective-permute-start.3
  172.0 1.8 collective-permute-done.3
  174.0 0.5 sqrt_bitcast_fusion
  (45 shorter events, 2.0 us)
Async XLA Ops:
  12.6 6.5 %copy-start = (f32[1,128,2]{1,2,0:T(2,128)S(1)}, f32[1,128,2]{1,2,0:T(2,128)}, u32[]{:S(2)}) copy-start(f32[1,128,2]{1,2,0:T(2,128)} %param.16) | copy-start | bytes 3076
  12.7 6.6 %copy-start.3 = (f32[3,1,128]{2,1,0:T(1,128)S(1)}, f32[3,1,128]{2,1,0:T(1,128)}, u32[]{:S(2)}) copy-start(f32[3,1,128]{2,1,0:T(1,128)} %param.17) | copy-start | bytes 4612
  12.7 66.6 %all-to-all-start = ((bf16[4,3,43,2304]{3,2,1,0:T(8,128)(2,1)}), bf16[4,3,43,2304]{3,2,1,0:T(8,128)(2,1)S(1)}, u32[]{:S(2)}, u32[]{:S(2)}) async-start(bf16[4,3,43,2304]{3,2,1,0:T(8,128)(2,1)} %reshape.146), calls=%async_computation | async-start | bytes 5308416 | tf_op jit(solution)/shard_map/all_to_all | solution.py:110
  119.7 9.0 %all-to-all-start.1 = ((bf16[4,2,4128]{2,1,0:T(2,128)(2,1)}), bf16[4,2,4128]{2,1,0:T(2,128)(2,1)S(1)}, u32[]{:S(2)}, u32[]{:S(2)}) async-start(bf16[4,2,4128]{2,1,0:T(2,128)(2,1)} %reshape.173), calls=%async_computation.1 | async-start | bytes 135168 | tf_op jit(solution)/shard_map/all_to_all | solution.py:131
  123.2 9.6 %copy-start.1 = (f32[3,3]{1,0:T(4,128)S(1)}, f32[3,3]{1,0:T(4,128)}, u32[]{:S(2)}) copy-start(f32[3,3]{1,0:T(4,128)} %constant.40.clone) | copy-start | bytes 112
  128.8 45.0 %copy-start.2 = (f32[3]{0:T(128)S(1)}, f32[3]{0:T(128)}, u32[]{:S(2)}) copy-start(f32[3]{0:T(128)} %constant.42.clone) | copy-start | bytes 40
  128.8 45.1 %copy-start.4 = (f32[3]{0:T(128)S(1)}, f32[3]{0:T(128)}, u32[]{:S(2)}) copy-start(f32[3]{0:T(128)} %constant.68.clone) | copy-start | bytes 40
  128.8 45.1 %copy-start.5 = (f32[3]{0:T(128)S(1)}, f32[3]{0:T(128)}, u32[]{:S(2)}) copy-start(f32[3]{0:T(128)} %constant.80) | copy-start | bytes 40
  133.0 36.3 %collective-permute-start = (f32[3,1,128]{2,0,1:T(4,128)S(1)}, f32[3,1,128]{2,0,1:T(4,128)S(1)}, u32[]{:S(2)}, u32[]{:S(2)}) collective-permute-start(f32[3,1,128]{2,0,1:T(4,128)S(1)} %convolution_bitcast_fusion), channel_id=1, source_target_pairs={{0,4},{4,8},{8,12},{1,5},{5,9},{9,13},{2,6},{6,10},{10,14},{3,7},{... | collective-permute-start | bytes 4616 | tf_op jit(solution)/shard_map/ppermute | solution.py:21
  135.8 33.5 %collective-permute-start.1 = (f32[3,1,128]{2,0,1:T(4,128)S(1)}, f32[3,1,128]{2,0,1:T(4,128)S(1)}, u32[]{:S(2)}, u32[]{:S(2)}) collective-permute-start(f32[3,1,128]{2,0,1:T(4,128)S(1)} %convolution_bitcast_fusion), channel_id=1, source_target_pairs={{4,0},{8,4},{12,8},{5,1},{9,5},{13,9},{6,2},{10,6},{14,10},{7,3},{... | collective-permute-start | bytes 4616 | tf_op jit(solution)/shard_map/ppermute | solution.py:24
  169.4 2.6 %collective-permute-start.2 = (f32[3,3,1]{2,0,1:T(4,128)S(1)}, f32[3,3,1]{2,0,1:T(4,128)S(1)}, u32[]{:S(2)}, u32[]{:S(2)}) collective-permute-start(f32[3,3,1]{2,0,1:T(4,128)S(1)} %get-tuple-element.61), channel_id=1, source_target_pairs={{0,1},{1,2},{2,3},{4,5},{5,6},{6,7},{8,9},{9,10},{10,11},{12,13},{... | collective-permute-start | bytes 116 | tf_op jit(solution)/shard_map/ppermute | solution.py:21
  170.7 3.1 %collective-permute-start.3 = (f32[3,3,1]{2,0,1:T(4,128)S(1)}, f32[3,3,1]{2,0,1:T(4,128)S(1)}, u32[]{:S(2)}, u32[]{:S(2)}) collective-permute-start(f32[3,3,1]{2,0,1:T(4,128)S(1)} %get-tuple-element.62), channel_id=1, source_target_pairs={{1,0},{2,1},{3,2},{5,4},{6,5},{7,6},{9,8},{10,9},{11,10},{13,12},{... | collective-permute-start | bytes 116 | tf_op jit(solution)/shard_map/ppermute | solution.py:24
where the time goes:
time: 178 us; the launch traced here: 176 us
  waiting for transfers between devices  67.2 us (38%)
  local copies, waits for them, and re-layouts  33.9 us (19%)
  blocking collectives  30.8 us (17%)
  matrix products  18.7 us (11%)
  starting transfers between devices  16.6 us (9%)
  other arithmetic  5.69 us (3%)
  between operations  2.74 us (2%)
    all_to_all x1, waiting for transfers between devices, body(): lax.all_to_all(encoded_slots.reshape(block_count, local_blocks, capacity,...  59.9 us
    psum x1, blocking collectives, body(): lax.psum(jnp.sum(difference * difference), ('block', 'rep', 'tile'))  30.8 us
    dot_general x3, matrix products, network(): jnp.dot(layer_one, weight_hidden, preferred_element_type=jnp.float32)  11.7 us
    reshape x1, local copies, waits for them, and re-layouts, body(): jnp.transpose(received, (1, 0, 2, 3))  9.26 us
    dynamic_slice x3, local copies, waits for them, and re-layouts, body(): lax.map(per_block_encoded, (input_rows, w_in, w_hid, w_out))  7.6 us
    dot_general x3, matrix products, network(): lax.dot_general(weight_out, layer_two, (((1,), (1,)), ((), ())), preferre...  6.89 us
    all_to_all x1, starting transfers between devices, body(): lax.all_to_all(encoded_slots.reshape(block_count, local_blocks, capacity,...  6.45 us
    all_to_all x1, waiting for transfers between devices, body(): lax.all_to_all(flattened.astype(jnp.bfloat16), 'block', split_axis=0, con...  5.51 us
  transfers between devices with their start and end apart: 6, of which 3 were waited for; matrix products, arithmetic and copies ran while one was open for 1% of the time, Pallas kernels for 0%

commit v1 on v0

v1 whole, which is shorter than its diff:
```python
import functools
import math

import jax
import jax.numpy as jnp
import ml_dtypes
import numpy as np
from jax import lax
from jax.experimental import pallas as pl
from jax.experimental.pallas import tpu as pltpu
from jax.sharding import PartitionSpec as P

RC = 128
DC = 16
NBINS = 256
TILE = 32
EXTRA = 32

OPPONENT = ((0.2126, 0.7152, 0.0722), (0.5, -0.5, 0.0), (0.0, 0.4, -0.4))
SPREAD = (0.6, 0.35, 0.35)
EMPHASIS = (1.0, 2.0, 2.0)

F32 = jnp.float32
BF16 = jnp.bfloat16
VMEM_LIMIT = 48 * 1024 * 1024


def iota(shape, dim):
    return lax.broadcasted_iota(jnp.int32, shape, dim)


def parts_of(values):
    high = values.astype(BF16).astype(F32)
    rest = values - high
    middle = rest.astype(BF16).astype(F32)
    return [high, middle, rest - middle]


def depth_table(sample_num):
    powers = np.arange(DC // 2, dtype=np.float32)
    steps = (np.float32(np.pi) * np.exp2(powers) / np.float32(NBINS)).astype(np.float32)
    angles = np.arange(NBINS, dtype=np.float32)[:, None] * steps
    wide = angles.astype(np.float64)
    code = np.concatenate([np.sin(wide), np.cos(wide)], axis=1).astype(np.float32)
    stride = NBINS // sample_num
    table = np.zeros((NBINS, sample_num, DC), np.float32)
    for row in range(NBINS):
        table[row, row // stride] = code[row]
    return table.reshape(NBINS, sample_num * DC).astype(ml_dtypes.bfloat16)


def pack_kernel(visible, bins, ray_code, blend, truth, message):
    pixels = ray_code.shape[0]
    message[0:pixels] = ray_code[...]
    lists = bins.shape[0] * bins.shape[1]
    message[pixels : pixels + lists] = bins[...].astype(F32).reshape(lists, pixels).astype(BF16)
    truths = truth[...].reshape(truth.shape[0], pixels)
    rows = [visible[...].astype(F32)] + parts_of(blend[...]) + parts_of(truths)
    used = sum(row.shape[0] for row in rows)
    rows.append(jnp.zeros((EXTRA - used, pixels), F32))
    message[pixels + lists :] = jnp.concatenate(rows, axis=0).astype(BF16)


def serve_kernel(sources, slots, *refs):
    messages = refs[:sources]
    w_in, w_hid, w_out, table, partial, aside = refs[sources : sources + 6]
    places, mixed, codes, depths, first_w, last_w, heads = refs[sources + 6 :]
    local_blocks, in_width, hidden = w_in.shape
    pixels = messages[0].shape[1]
    lists = messages[0].shape[0] - pixels - EXTRA
    samples = lists // 2
    first_block = lax.axis_index("block") * local_blocks

    extras = [messages[s][pixels + lists :].astype(F32) for s in range(sources)]

    named = []
    for s in range(sources):
        for v in range(2):
            own = iota((8, pixels), 0) + first_block
            hit = (extras[s][v : v + 1] == own.astype(F32)) & (iota((8, pixels), 0) < local_blocks)
            named.append(hit.astype(F32))
    either = [named[2 * s] + named[2 * s + 1] for s in range(sources)]
    before = (iota((pixels, pixels), 0) < iota((pixels, pixels), 1)).astype(F32).astype(BF16)
    ranks = jnp.dot(
        jnp.concatenate(either, axis=0).astype(BF16), before, preferred_element_type=F32
    )
    offset = jnp.zeros((8, 1), F32)
    slot_row = iota((slots, pixels), 0).astype(F32)
    for s in range(sources):
        rank = ranks[8 * s : 8 * s + 8] + offset
        offset = offset + jnp.sum(either[s], axis=1, keepdims=True)
        for v in range(2):
            spot = jnp.where(named[2 * s + v] > 0.0, rank, -1.0)
            lanes = pl.ds((2 * s + v) * pixels, pixels)
            for k in range(local_blocks):
                places[k * slots : (k + 1) * slots, lanes] = (
                    (slot_row == spot[k : k + 1]).astype(F32).astype(BF16)
                )
    tiles = [
        (jnp.max(offset[k : k + 1]).astype(jnp.int32) + TILE - 1) // TILE
        for k in range(local_blocks)
    ]

    lane = iota((pixels, pixels), 1)
    per_turn = pixels // lists
    for turn in range(0, sources, per_turn):
        group = [
            messages[s][pixels : pixels + lists].astype(F32)
            for s in range(turn, min(turn + per_turn, sources))
        ]
        if len(group) < per_turn:
            group.append(jnp.zeros(((per_turn - len(group)) * lists, pixels), F32))
        turned = jnp.concatenate(group, axis=0).T
        for s in range(turn, min(turn + per_turn, sources)):
            for v in range(2):
                rows = pl.ds((2 * s + v) * pixels, pixels)
                mine = lane // samples == 2 * (s - turn) + v
                mixed[rows, 0:RC] = messages[s][0:pixels]
                mixed[rows, RC:] = jnp.where(mine, turned, 0.0).astype(BF16)

    chosen = jnp.dot(places[...], mixed[...], preferred_element_type=F32).astype(BF16)
    codes[...] = chosen[:, :RC]
    spread_shape = (pixels, samples * DC)
    spread = (iota(spread_shape, 0) % samples == iota(spread_shape, 1) // DC).astype(F32)
    bins = jnp.dot(chosen[:, RC:], spread.astype(BF16), preferred_element_type=F32)
    is_bin = (bins == iota(bins.shape, 1).astype(F32)).astype(F32).astype(BF16)
    depths[...] = jnp.dot(is_bin, table[...], preferred_element_type=F32).astype(BF16)

    heads[...] = jnp.zeros_like(heads)
    per_half = RC // DC
    for k in range(local_blocks):
        first_w[0:RC] = w_in[k, 0:RC]
        for i in range(per_half):
            first_w[RC + i * DC : RC + (i + 1) * DC] = w_in[k, RC:]
        wide = jnp.concatenate(
            [jnp.broadcast_to(w_out[k, c : c + 1].astype(F32), (samples, hidden)) for c in range(4)]
            + [jnp.zeros((128 - 4 * samples, hidden), F32)],
            axis=0,
        )
        last_w[...] = wide.T.astype(BF16)

        def one_tile(t, carry, k=k):
            rows = pl.ds(pl.multiple_of(k * slots + t * TILE, TILE), TILE)
            code = codes[rows, :]
            depth = depths[rows, :]
            half_lane = iota((TILE, RC), 1) // DC
            inputs = []
            for j in range(samples):
                half = depth[:, (j // per_half) * RC : (j // per_half + 1) * RC]
                kept = jnp.where(half_lane == j % per_half, half, jnp.zeros_like(half))
                inputs.append(jnp.concatenate([code, kept], axis=1))
            inputs = jnp.concatenate(inputs, axis=0)
            one = jnp.dot(inputs, first_w[...], preferred_element_type=F32)
            one = jnp.maximum(one, 0.0).astype(BF16)
            two = jnp.dot(one, w_hid[k], preferred_element_type=F32)
            two = jnp.maximum(two, 0.0).astype(BF16)
            out = jnp.dot(two, last_w[...], preferred_element_type=F32)
            sample_lane = iota((TILE, 128), 1) % samples
            total = jnp.zeros((TILE, 128), F32)
            for j in range(samples):
                total = jnp.where(sample_lane == j, out[j * TILE : (j + 1) * TILE], total)
            heads[rows, :] = total
            return carry

        lax.fori_loop(0, tiles[k], one_tile, 0)

    turned = heads[...].T
    optical = jax.nn.softplus(turned[0:samples]) * (1.5 / samples)
    lower = (iota((samples, samples), 1) < iota((samples, samples), 0)).astype(F32)
    ahead = jnp.dot(
        jnp.concatenate([lower] * 3, axis=1).astype(BF16),
        jnp.concatenate(parts_of(optical), axis=0).astype(BF16),
        preferred_element_type=F32,
    )
    weights = jnp.exp(-ahead) * (1.0 - jnp.exp(-optical))
    background = 1.0 - jnp.sum(weights, axis=0, keepdims=True)
    shades = []
    for c in range(1, 4):
        color = jax.nn.sigmoid(turned[c * samples : (c + 1) * samples])
        shades.append(jnp.sum(weights * color, axis=0, keepdims=True) + background)
    shades.append(jnp.zeros_like(background))
    shades = jnp.concatenate(shades, axis=0)[:, : local_blocks * slots]
    stacked = jnp.concatenate(parts_of(shades) + [jnp.zeros_like(shades)], axis=0).astype(BF16)
    spots = jnp.dot(stacked, places[...], preferred_element_type=F32)
    spots = spots[0:4] + spots[4:8] + spots[8:12]
    for s in range(sources):
        blend = [extras[s][2 + v : 3 + v] + extras[s][4 + v : 5 + v] + extras[s][6 + v : 7 + v] for v in range(2)]
        lanes = slice(s * pixels, (s + 1) * pixels)
        mine = [spots[:, (2 * s + v) * pixels : (2 * s + v + 1) * pixels] * blend[v] for v in range(2)]
        partial[:, lanes] = mine[0] + mine[1]
        aside[0:3, lanes] = extras[s][8:11] + extras[s][11:14] + extras[s][14:17]
        aside[3:4, lanes] = blend[0] + blend[1]


def gather_kernel(sources, *refs):
    partials = refs[:sources]
    aside, rendered, message = refs[sources:]
    pixels = rendered.shape[2]
    z = lax.axis_index("block")

    def block(ref, u):
        return ref[:, u * pixels : (u + 1) * pixels]

    squared = jnp.zeros((3, pixels), F32)
    rows = []
    for u in range(sources):
        total = block(partials[0], u)
        for t in range(1, sources):
            total = total + block(partials[t], t ^ u)
        extra = block(aside, u)
        shown = total[0:3] / extra[3:4]
        if u == 0:
            rendered[...] = shown.reshape(3, 1, pixels)
        difference = shown - extra[0:3]
        squared = squared + difference * difference
        rows.append(difference)
    above = jnp.zeros((3, pixels), F32)
    below = jnp.zeros((3, pixels), F32)
    for u in range(1, sources):
        above = above + jnp.where((z ^ u) == z - 1, rows[u], 0.0)
        below = below + jnp.where((z ^ u) == z + 1, rows[u], 0.0)
    for c in range(3):
        def channel(d):
            return sum(OPPONENT[c][i] * d[i : i + 1] for i in range(3) if OPPONENT[c][i])

        message[c : c + 1] = SPREAD[c] * channel(above) + channel(rows[0]) + SPREAD[c] * channel(below)
    total = jnp.sum(jnp.sum(squared, axis=0, keepdims=True), axis=1, keepdims=True)
    message[3:4] = jnp.broadcast_to(total, (1, pixels))


def finish_kernel(columns, count, *refs):
    messages = refs[:columns]
    flip_map, psnr = refs[columns:]
    pixels = flip_map.shape[1]
    q = lax.axis_index("rep") * lax.axis_size("tile") + lax.axis_index("tile")
    own = messages[0][...]
    left = jnp.zeros_like(own)
    right = jnp.zeros_like(own)
    total = own[3:4]
    for s in range(1, columns):
        other = messages[s][...]
        left = left + jnp.where((q ^ s) == q - 1, other, 0.0)
        right = right + jnp.where((q ^ s) == q + 1, other, 0.0)
        total = total + other[3:4]
    lane = iota(own.shape, 1)
    before = pltpu.roll(jnp.where(lane == pixels - 1, left, own), 1, 1)
    after = pltpu.roll(jnp.where(lane == 0, right, own), pixels - 1, 1)
    summed = jnp.zeros((1, pixels), F32)
    for c in range(3):
        column = SPREAD[c] * before[c : c + 1] + own[c : c + 1] + SPREAD[c] * after[c : c + 1]
        scale = np.float32(1.0) + np.float32(2.0) * np.float32(SPREAD[c])
        filtered = column / float(scale * scale)
        emphasised = EMPHASIS[c] * filtered
        summed = summed + emphasised * emphasised
    flip_map[...] = jnp.sqrt(summed + 1e-06)
    logged = jnp.log(total / count + 1e-06) * (-10.0 / math.log(10.0))
    psnr[...] = logged[:, 0:1]


def exchange(value, axes, size):
    out = [value]
    for s in range(1, size):
        out.append(lax.ppermute(value, axes, [(i, i ^ s) for i in range(size)]))
    return out


def call(kernel, out_shape, scratch=(), flops=0, bytes_accessed=0):
    return pl.pallas_call(
        kernel,
        out_shape=out_shape,
        scratch_shapes=list(scratch),
        compiler_params=pltpu.CompilerParams(vmem_limit_bytes=VMEM_LIMIT),
    )


def body(visible, bins, ray_code, blend, truth, w_in, w_hid, w_out):
    sources = lax.axis_size("block")
    columns = lax.axis_size("rep") * lax.axis_size("tile")
    local_blocks, in_width, hidden = w_in.shape
    pixels = visible.shape[1]
    visible_num = visible.shape[2]
    samples = bins.shape[3]
    blocks_all = local_blocks * sources
    capacity = (2 * pixels * visible_num + blocks_all - 1) // blocks_all
    slots = -(-sources * capacity // TILE) * TILE
    slots_all = local_blocks * slots
    lists = visible_num * samples
    height = pixels + lists + EXTRA

    message = call(pack_kernel, jax.ShapeDtypeStruct((height, pixels), BF16))(
        visible.reshape(pixels, visible_num).T,
        jnp.transpose(bins.reshape(pixels, visible_num, samples), (1, 2, 0)),
        ray_code.reshape(pixels, RC),
        blend.reshape(pixels, visible_num).T,
        truth,
    )
    messages = exchange(message, "block", sources)
    partial, aside = call(
        functools.partial(serve_kernel, sources, slots),
        (
            jax.ShapeDtypeStruct((4, sources * pixels), F32),
            jax.ShapeDtypeStruct((4, sources * pixels), F32),
        ),
        (
            pltpu.VMEM((slots_all, sources * visible_num * pixels), BF16),
            pltpu.VMEM((sources * visible_num * pixels, 2 * RC), BF16),
            pltpu.VMEM((slots_all, RC), BF16),
            pltpu.VMEM((slots_all, samples * DC), BF16),
            pltpu.VMEM((2 * RC, hidden), BF16),
            pltpu.VMEM((hidden, 128), BF16),
            pltpu.VMEM((-(-slots_all // 128) * 128, 128), F32),
        ),
    )(*messages, w_in, w_hid, w_out, jnp.asarray(depth_table(samples)))
    partials = exchange(partial, "block", sources)
    rendered, edge = call(
        functools.partial(gather_kernel, sources),
        (
            jax.ShapeDtypeStruct((3, 1, pixels), F32),
            jax.ShapeDtypeStruct((4, pixels), F32),
        ),
    )(*partials, aside)
    edges = exchange(edge, ("rep", "tile"), columns)
    flip_map, psnr = call(
        functools.partial(finish_kernel, columns, 3 * sources * columns * pixels),
        (
            jax.ShapeDtypeStruct((1, pixels), F32),
            jax.ShapeDtypeStruct((1, 1), F32),
        ),
    )(*edges)
    return (rendered, flip_map, psnr.reshape(1))


def solution(mesh):
    placed = (
        P(("groups", "block"), ("rep", "tile"), None),
        P(("groups", "block"), ("rep", "tile"), None, None),
        P(("groups", "block"), ("rep", "tile"), None),
        P(("groups", "block"), ("rep", "tile"), None),
        P(None, ("groups", "block"), ("rep", "tile")),
        P("block", None, None),
        P("block", None, None),
        P("block", None, None),
    )
    return jax.shard_map(
        body,
        mesh=mesh,
        in_specs=placed,
        out_specs=(
            P(None, ("groups", "block"), ("rep", "tile")),
            P(("groups", "block"), ("rep", "tile")),
            P("groups"),
        ),
        check_vma=False,
    )
```

time: 178 us -> 42.2 us (0.24); the launches traced: 176 us -> 42.4 us
  waiting for transfers between devices: 67.2 us -> 7.73 us
  blocking collectives: 30.8 us -> 0 us
  local copies, waits for them, and re-layouts: 33.9 us -> 7.54 us
  matrix products: 18.7 us -> 0 us
  Pallas kernels: 0 us -> 14.4 us
  other arithmetic: 5.69 us -> 0 us
  starting transfers between devices: 16.6 us -> 12 us
  between operations: 2.74 us -> 0.68 us
    all_to_all x2 -> x0, waiting for transfers between devices: 65.4 us -> none  [the longest x1 59.9 us: body(): lax.all_to_all(encoded_slots.reshape(block_count, local_blocks, capacity,...]
    psum x1 -> x0, blocking collectives: 30.8 us -> none  [body(): lax.psum(jnp.sum(difference * difference), ('block', 'rep', 'tile'))]
    dot_general x7 -> x0, matrix products: 18.7 us -> none  [the longest x3 11.7 us: network(): jnp.dot(layer_one, weight_hidden, preferred_element_type=jnp.float32)]
    pallas_call x0 -> x4, Pallas kernels: none -> 14.4 us  [the longest x1 13.2 us: body(): call(functools.partial(serve_kernel, sources, slots), (jax.ShapeDtypeStru...]
    reshape x3 -> x0, local copies, waits for them, and re-layouts: 12.8 us -> none  [the longest x1 9.26 us: body(): jnp.transpose(received, (1, 0, 2, 3))]
    all_to_all x2 -> x0, starting transfers between devices: 9.91 us -> none  [the longest x1 6.45 us: body(): lax.all_to_all(encoded_slots.reshape(block_count, local_blocks, capacity,...]
    dynamic_slice x3 -> x0, local copies, waits for them, and re-layouts: 7.6 us -> none  [body(): lax.map(per_block_encoded, (input_rows, w_in, w_hid, w_out))]
    ppermute x4 -> x9, waiting for transfers between devices: 1.76 us -> 7.73 us  [exchange(): out.append(lax.ppermute(value, axes, [(i, i ^ s) for i in range(size)]))]
  transfers between devices with their start and end apart: 6 -> 9, of which waited for: 3 -> 6; matrix products, arithmetic and copies ran while one was open for 1% -> 0% of each run, Pallas kernels for 0% -> 0%
where the time goes in v1:
time: 42.2 us; the launch traced here: 42.4 us
  Pallas kernels  14.4 us (34%)
  starting transfers between devices  12 us (28%)
  waiting for transfers between devices  7.73 us (18%)
  local copies, waits for them, and re-layouts  7.54 us (18%)
  between operations  0.68 us (2%)
    pallas_call x1, Pallas kernels, body(): call(functools.partial(serve_kernel, sources, slots), (jax.ShapeDtypeStru...  13.2 us
    ppermute x9, starting transfers between devices, exchange(): out.append(lax.ppermute(value, axes, [(i, i ^ s) for i in range(size)]))  12 us
    ppermute x9, waiting for transfers between devices, exchange(): out.append(lax.ppermute(value, axes, [(i, i ^ s) for i in range(size)]))  7.73 us
    unnamed x18, local copies, waits for them, and re-layouts  7.54 us
  transfers between devices with their start and end apart: 9, of which 6 were waited for; matrix products, arithmetic and copies ran while one was open for 0% of the time, Pallas kernels for 0%

profile of v1, /device:TPU:0, one launch (start us, length us, event | category | flops | bytes accessed | tf_op | source)
XLA Modules:
  0.0 42.4 jit_solution(17808250132059024113)
XLA Ops:
  0.6 0.0 copy-start.3
  0.6 0.7 %copy-done.3 = bf16[1,128,128]{2,1,0:T(8,128)(2,1)S(1)} copy-done((bf16[1,128,128]{2,1,0:T(8,128)(2,1)S(1)}, bf16[1,128,128]{2,1,0:T(8,128)(2,1)}, u32[]{:S(2)}) %copy-start.3) | copy-done | bytes 32792
  1.4 0.0 copy-start.4
  1.4 0.7 %copy-done.4 = s32[1,128,2,16]{1,3,2,0:T(8,128)S(1)} copy-done((s32[1,128,2,16]{1,3,2,0:T(8,128)S(1)}, s32[1,128,2,16]{1,3,2,0:T(8,128)}, u32[]{:S(2)}) %copy-start.4) | copy-done | bytes 16408
  2.1 0.0 copy-start.6
  2.1 0.7 %copy-done.6 = f32[3,1,128]{2,1,0:T(1,128)S(1)} copy-done((f32[3,1,128]{2,1,0:T(1,128)S(1)}, f32[3,1,128]{2,1,0:T(1,128)}, u32[]{:S(2)}) %copy-start.6) | copy-done | bytes 1560
  2.8 0.0 copy-start.7
  2.8 0.7 %copy-done.7 = s32[1,128,2]{1,2,0:T(2,128)S(1)} copy-done((s32[1,128,2]{1,2,0:T(2,128)S(1)}, s32[1,128,2]{1,2,0:T(2,128)}, u32[]{:S(2)}) %copy-start.7) | copy-done | bytes 1048
  3.5 0.0 copy-start.8
  3.5 0.7 %copy-done.8 = f32[1,128,2]{1,2,0:T(2,128)S(1)} copy-done((f32[1,128,2]{1,2,0:T(2,128)S(1)}, f32[1,128,2]{1,2,0:T(2,128)}, u32[]{:S(2)}) %copy-start.8) | copy-done | bytes 1048
  4.2 5.1 %collective-permute-start.2 = (bf16[192,128]{1,0:T(8,128)(2,1)S(1)}, bf16[192,128]{1,0:T(8,128)(2,1)S(1)}, u32[]{:S(2)}, u32[]{:S(2)}) collective-permute-start(bf16[192,128]{1,0:T(8,128)(2,1)S(1)} %shard_map.112.refs_0_), channel_id=1, source_target_pairs={{0,12},{4,8},{8,4},{12,0},{1,13},{5,9},{9,5},{13,1},{2,14},{6,10},... | collective-permute-start | bytes 147464 | tf_op jit(solution)/shard_map/ppermute | solution.py:263
  9.3 0.0 collective-permute-start.1
  9.3 0.6 %collective-permute-start = (bf16[192,128]{1,0:T(8,128)(2,1)S(1)}, bf16[192,128]{1,0:T(8,128)(2,1)S(1)}, u32[]{:S(2)}, u32[]{:S(2)}) collective-permute-start(bf16[192,128]{1,0:T(8,128)(2,1)S(1)} %shard_map.112.refs_0_), channel_id=1, source_target_pairs={{0,4},{4,0},{8,12},{12,8},{1,5},{5,1},{9,13},{13,9},{2,6},{6,2},{1... | collective-permute-start | bytes 147464 | tf_op jit(solution)/shard_map/ppermute | solution.py:263
  9.9 1.6 %collective-permute-done.2.refs_3_ = bf16[192,128]{1,0:T(8,128)(2,1)S(1)} collective-permute-done((bf16[192,128]{1,0:T(8,128)(2,1)S(1)}, bf16[192,128]{1,0:T(8,128)(2,1)S(1)}, u32[]{:S(2)}, u32[]{:S(2)}) %collective-permute-start.2) | collective-permute-done | bytes 49184 | tf_op jit(solution)/shard_map/ppermute | solution.py:263
  11.5 2.8 %collective-permute-done.1.refs_2_ = bf16[192,128]{1,0:T(8,128)(2,1)S(1)} collective-permute-done((bf16[192,128]{1,0:T(8,128)(2,1)S(1)}, bf16[192,128]{1,0:T(8,128)(2,1)S(1)}, u32[]{:S(2)}, u32[]{:S(2)}) %collective-permute-start.1) | collective-permute-done | bytes 49184 | tf_op jit(solution)/shard_map/ppermute | solution.py:263
  14.3 0.0 collective-permute-done.refs_1_
  14.3 0.0 copy-start
  14.3 1.4 %copy-done = bf16[3,512,512]{2,1,0:T(8,128)(2,1)S(1)} copy-done((bf16[3,512,512]{2,1,0:T(8,128)(2,1)S(1)}, bf16[3,512,512]{2,1,0:T(8,128)(2,1)}, u32[]{:S(2)}) %copy-start) | copy-done | bytes 1572888
  15.7 0.0 copy-start.1
  15.7 1.0 %copy-done.1 = bf16[3,144,512]{2,1,0:T(8,128)(2,1)S(1)} copy-done((bf16[3,144,512]{2,1,0:T(8,128)(2,1)S(1)}, bf16[3,144,512]{2,1,0:T(8,128)(2,1)}, u32[]{:S(2)}) %copy-start.1) | copy-done | bytes 442392
  16.7 0.0 copy-start.2
  16.7 0.9 %copy-done.2 = bf16[256,256]{1,0:T(8,128)(2,1)S(1)} copy-done((bf16[256,256]{1,0:T(8,128)(2,1)S(1)}, bf16[256,256]{1,0:T(8,128)(2,1)}, u32[]{:S(2)}) %copy-start.2) | copy-done | bytes 131096
  17.6 0.0 copy-start.5
  17.6 0.7 %copy-done.5 = bf16[3,4,512]{2,1,0:T(4,128)(2,1)S(1)} copy-done((bf16[3,4,512]{2,1,0:T(4,128)(2,1)S(1)}, bf16[3,4,512]{2,1,0:T(4,128)(2,1)}, u32[]{:S(2)}) %copy-start.5) | copy-done | bytes 12312
  18.3 13.2 %shard_map.113 = (f32[4,512]{1,0:T(4,128)S(1)}, f32[4,512]{1,0:T(4,128)S(1)}) custom-call(bf16[192,128]{1,0:T(8,128)(2,1)S(1)} %shard_map.112.refs_0_, bf16[192,128]{1,0:T(8,128)(2,1)S(1)} %collective-permute-done.refs_1_, bf16[192,128]{1,0:T(8,128)(2,1)S(1)} %collective-permute-done.1.refs_2_, bf16[192,128]{1,0:T(8,128)(2,1)S(1)} %collective-permute-done.2.refs_3_, ...), custom_call_target="tpu_custom_call" | custom-call | tf_op jit(solution)/shard_map/pallas_call | solution.py:298
  31.5 0.0 collective-permute-start.5
  31.6 0.1 collective-permute-start.4
  31.6 4.3 %collective-permute-start.3 = (f32[4,512]{1,0:T(4,128)S(1)}, f32[4,512]{1,0:T(4,128)S(1)}, u32[]{:S(2)}, u32[]{:S(2)}) collective-permute-start(f32[4,512]{1,0:T(4,128)S(1)} %get-tuple-element.9.refs_0_), channel_id=1, source_target_pairs={{0,4},{4,0},{8,12},{12,8},{1,5},{5,1},{9,13},{13,9},{2,6},{6,2},{1... | collective-permute-start | bytes 24584 | tf_op jit(solution)/shard_map/ppermute | solution.py:263
  35.9 1.1 %collective-permute-done.5.refs_3_ = f32[4,512]{1,0:T(4,128)S(1)} collective-permute-done((f32[4,512]{1,0:T(4,128)S(1)}, f32[4,512]{1,0:T(4,128)S(1)}, u32[]{:S(2)}, u32[]{:S(2)}) %collective-permute-start.5) | collective-permute-done | bytes 8224 | tf_op jit(solution)/shard_map/ppermute | solution.py:263
  37.0 0.0 collective-permute-done.4.refs_2_
  37.0 0.6 %collective-permute-done.3.refs_1_ = f32[4,512]{1,0:T(4,128)S(1)} collective-permute-done((f32[4,512]{1,0:T(4,128)S(1)}, f32[4,512]{1,0:T(4,128)S(1)}, u32[]{:S(2)}, u32[]{:S(2)}) %collective-permute-start.3) | collective-permute-done | bytes 8224 | tf_op jit(solution)/shard_map/ppermute | solution.py:263
  37.6 0.6 %shard_map.114 = (f32[3,1,128]{2,1,0:T(1,128)}, f32[4,128]{1,0:T(4,128)S(1)}) custom-call(f32[4,512]{1,0:T(4,128)S(1)} %get-tuple-element.9.refs_0_, f32[4,512]{1,0:T(4,128)S(1)} %collective-permute-done.3.refs_1_, f32[4,512]{1,0:T(4,128)S(1)} %collective-permute-done.4.refs_2_, f32[4,512]{1,0:T(4,128)S(1)} %collective-permute-done.5.refs_3_, ...), custom_call_target="tpu_custom_call" | custom-call | tf_op jit(solution)/shard_map/pallas_call | solution.py:315
  38.1 0.0 collective-permute-start.8
  38.1 0.7 %collective-permute-start.7 = (f32[4,128]{1,0:T(4,128)S(1)}, f32[4,128]{1,0:T(4,128)S(1)}, u32[]{:S(2)}, u32[]{:S(2)}) collective-permute-start(f32[4,128]{1,0:T(4,128)S(1)} %get-tuple-element.12.refs_0_), channel_id=1, source_target_pairs={{0,2},{1,3},{2,0},{3,1},{4,6},{5,7},{6,4},{7,5},{8,10},{9,11},{10,... | collective-permute-start | bytes 6152 | tf_op jit(solution)/shard_map/ppermute | solution.py:263
  38.8 1.2 %collective-permute-start.6 = (f32[4,128]{1,0:T(4,128)S(1)}, f32[4,128]{1,0:T(4,128)S(1)}, u32[]{:S(2)}, u32[]{:S(2)}) collective-permute-start(f32[4,128]{1,0:T(4,128)S(1)} %get-tuple-element.12.refs_0_), channel_id=1, source_target_pairs={{0,1},{1,0},{2,3},{3,2},{4,5},{5,4},{6,7},{7,6},{8,9},{9,8},{10,11... | collective-permute-start | bytes 6152 | tf_op jit(solution)/shard_map/ppermute | solution.py:263
  40.0 1.1 %collective-permute-done.8.refs_3_ = f32[4,128]{1,0:T(4,128)S(1)} collective-permute-done((f32[4,128]{1,0:T(4,128)S(1)}, f32[4,128]{1,0:T(4,128)S(1)}, u32[]{:S(2)}, u32[]{:S(2)}) %collective-permute-start.8) | collective-permute-done | bytes 2080 | tf_op jit(solution)/shard_map/ppermute | solution.py:263
  41.1 0.6 %collective-permute-done.7.refs_2_ = f32[4,128]{1,0:T(4,128)S(1)} collective-permute-done((f32[4,128]{1,0:T(4,128)S(1)}, f32[4,128]{1,0:T(4,128)S(1)}, u32[]{:S(2)}, u32[]{:S(2)}) %collective-permute-start.7) | collective-permute-done | bytes 2080 | tf_op jit(solution)/shard_map/ppermute | solution.py:263
  41.8 0.0 collective-permute-done.6.refs_1_
  41.8 0.6 %shard_map.115 = (f32[1,128]{1,0:T(1,128)}, f32[1,1]{1,0:T(1,128)}) custom-call(f32[4,128]{1,0:T(4,128)S(1)} %get-tuple-element.12.refs_0_, f32[4,128]{1,0:T(4,128)S(1)} %collective-permute-done.6.refs_1_, f32[4,128]{1,0:T(4,128)S(1)} %collective-permute-done.7.refs_2_, f32[4,128]{1,0:T(4,128)S(1)} %collective-permute-done.8.refs_3_), custom_call_target="tpu_custom_call" | custom-call | tf_op jit(solution)/shard_map/pallas_call | solution.py:323
  (1 shorter events, 0.0 us)
Async XLA Ops:
  0.6 0.8 %copy-start.3 = (bf16[1,128,128]{2,1,0:T(8,128)(2,1)S(1)}, bf16[1,128,128]{2,1,0:T(8,128)(2,1)}, u32[]{:S(2)}) copy-start(bf16[1,128,128]{2,1,0:T(8,128)(2,1)} %param.11) | copy-start | bytes 98308
  1.4 0.7 %copy-start.4 = (s32[1,128,2,16]{1,3,2,0:T(8,128)S(1)}, s32[1,128,2,16]{1,3,2,0:T(8,128)}, u32[]{:S(2)}) copy-start(s32[1,128,2,16]{1,3,2,0:T(8,128)} %param.10) | copy-start | bytes 49156
  2.1 0.7 %copy-start.6 = (f32[3,1,128]{2,1,0:T(1,128)S(1)}, f32[3,1,128]{2,1,0:T(1,128)}, u32[]{:S(2)}) copy-start(f32[3,1,128]{2,1,0:T(1,128)} %truth.1) | copy-start | bytes 4612
  2.8 0.7 %copy-start.7 = (s32[1,128,2]{1,2,0:T(2,128)S(1)}, s32[1,128,2]{1,2,0:T(2,128)}, u32[]{:S(2)}) copy-start(s32[1,128,2]{1,2,0:T(2,128)} %param.9) | copy-start | bytes 3076
  3.5 0.7 %copy-start.8 = (f32[1,128,2]{1,2,0:T(2,128)S(1)}, f32[1,128,2]{1,2,0:T(2,128)}, u32[]{:S(2)}) copy-start(f32[1,128,2]{1,2,0:T(2,128)} %param.12) | copy-start | bytes 3076
  4.2 7.3 %collective-permute-start.2 = (bf16[192,128]{1,0:T(8,128)(2,1)S(1)}, bf16[192,128]{1,0:T(8,128)(2,1)S(1)}, u32[]{:S(2)}, u32[]{:S(2)}) collective-permute-start(bf16[192,128]{1,0:T(8,128)(2,1)S(1)} %shard_map.112.refs_0_), channel_id=1, source_target_pairs={{0,12},{4,8},{8,4},{12,0},{1,13},{5,9},{9,5},{13,1},{2,14},{6,10},... | collective-permute-start | bytes 147464 | tf_op jit(solution)/shard_map/ppermute | solution.py:263
  9.3 5.0 %collective-permute-start.1 = (bf16[192,128]{1,0:T(8,128)(2,1)S(1)}, bf16[192,128]{1,0:T(8,128)(2,1)S(1)}, u32[]{:S(2)}, u32[]{:S(2)}) collective-permute-start(bf16[192,128]{1,0:T(8,128)(2,1)S(1)} %shard_map.112.refs_0_), channel_id=1, source_target_pairs={{0,8},{4,12},{8,0},{12,4},{1,9},{5,13},{9,1},{13,5},{2,10},{6,14},... | collective-permute-start | bytes 147464 | tf_op jit(solution)/shard_map/ppermute | solution.py:263
  9.3 5.0 %collective-permute-start = (bf16[192,128]{1,0:T(8,128)(2,1)S(1)}, bf16[192,128]{1,0:T(8,128)(2,1)S(1)}, u32[]{:S(2)}, u32[]{:S(2)}) collective-permute-start(bf16[192,128]{1,0:T(8,128)(2,1)S(1)} %shard_map.112.refs_0_), channel_id=1, source_target_pairs={{0,4},{4,0},{8,12},{12,8},{1,5},{5,1},{9,13},{13,9},{2,6},{6,2},{1... | collective-permute-start | bytes 147464 | tf_op jit(solution)/shard_map/ppermute | solution.py:263
  14.3 1.4 %copy-start = (bf16[3,512,512]{2,1,0:T(8,128)(2,1)S(1)}, bf16[3,512,512]{2,1,0:T(8,128)(2,1)}, u32[]{:S(2)}) copy-start(bf16[3,512,512]{2,1,0:T(8,128)(2,1)} %refs_5_.1) | copy-start | bytes 4718596
  15.7 1.0 %copy-start.1 = (bf16[3,144,512]{2,1,0:T(8,128)(2,1)S(1)}, bf16[3,144,512]{2,1,0:T(8,128)(2,1)}, u32[]{:S(2)}) copy-start(bf16[3,144,512]{2,1,0:T(8,128)(2,1)} %refs_4_.1) | copy-start | bytes 1327108
  16.7 0.9 %copy-start.2 = (bf16[256,256]{1,0:T(8,128)(2,1)S(1)}, bf16[256,256]{1,0:T(8,128)(2,1)}, u32[]{:S(2)}) copy-start(bf16[256,256]{1,0:T(8,128)(2,1)} %constant.2.clone.refs_7_) | copy-start | bytes 393220
  17.6 0.7 %copy-start.5 = (bf16[3,4,512]{2,1,0:T(4,128)(2,1)S(1)}, bf16[3,4,512]{2,1,0:T(4,128)(2,1)}, u32[]{:S(2)}) copy-start(bf16[3,4,512]{2,1,0:T(4,128)(2,1)} %refs_6_.1) | copy-start | bytes 36868
  31.5 5.5 %collective-permute-start.5 = (f32[4,512]{1,0:T(4,128)S(1)}, f32[4,512]{1,0:T(4,128)S(1)}, u32[]{:S(2)}, u32[]{:S(2)}) collective-permute-start(f32[4,512]{1,0:T(4,128)S(1)} %get-tuple-element.9.refs_0_), channel_id=1, source_target_pairs={{0,12},{4,8},{8,4},{12,0},{1,13},{5,9},{9,5},{13,1},{2,14},{6,10},... | collective-permute-start | bytes 24584 | tf_op jit(solution)/shard_map/ppermute | solution.py:263
  31.6 5.4 %collective-permute-start.4 = (f32[4,512]{1,0:T(4,128)S(1)}, f32[4,512]{1,0:T(4,128)S(1)}, u32[]{:S(2)}, u32[]{:S(2)}) collective-permute-start(f32[4,512]{1,0:T(4,128)S(1)} %get-tuple-element.9.refs_0_), channel_id=1, source_target_pairs={{0,8},{4,12},{8,0},{12,4},{1,9},{5,13},{9,1},{13,5},{2,10},{6,14},... | collective-permute-start | bytes 24584 | tf_op jit(solution)/shard_map/ppermute | solution.py:263
  31.6 5.9 %collective-permute-start.3 = (f32[4,512]{1,0:T(4,128)S(1)}, f32[4,512]{1,0:T(4,128)S(1)}, u32[]{:S(2)}, u32[]{:S(2)}) collective-permute-start(f32[4,512]{1,0:T(4,128)S(1)} %get-tuple-element.9.refs_0_), channel_id=1, source_target_pairs={{0,4},{4,0},{8,12},{12,8},{1,5},{5,1},{9,13},{13,9},{2,6},{6,2},{1... | collective-permute-start | bytes 24584 | tf_op jit(solution)/shard_map/ppermute | solution.py:263
  38.1 3.0 %collective-permute-start.8 = (f32[4,128]{1,0:T(4,128)S(1)}, f32[4,128]{1,0:T(4,128)S(1)}, u32[]{:S(2)}, u32[]{:S(2)}) collective-permute-start(f32[4,128]{1,0:T(4,128)S(1)} %get-tuple-element.12.refs_0_), channel_id=1, source_target_pairs={{0,3},{1,2},{2,1},{3,0},{4,7},{5,6},{6,5},{7,4},{8,11},{9,10},{10,... | collective-permute-start | bytes 6152 | tf_op jit(solution)/shard_map/ppermute | solution.py:263
  38.1 3.6 %collective-permute-start.7 = (f32[4,128]{1,0:T(4,128)S(1)}, f32[4,128]{1,0:T(4,128)S(1)}, u32[]{:S(2)}, u32[]{:S(2)}) collective-permute-start(f32[4,128]{1,0:T(4,128)S(1)} %get-tuple-element.12.refs_0_), channel_id=1, source_target_pairs={{0,2},{1,3},{2,0},{3,1},{4,6},{5,7},{6,4},{7,5},{8,10},{9,11},{10,... | collective-permute-start | bytes 6152 | tf_op jit(solution)/shard_map/ppermute | solution.py:263
  38.8 2.9 %collective-permute-start.6 = (f32[4,128]{1,0:T(4,128)S(1)}, f32[4,128]{1,0:T(4,128)S(1)}, u32[]{:S(2)}, u32[]{:S(2)}) collective-permute-start(f32[4,128]{1,0:T(4,128)S(1)} %get-tuple-element.12.refs_0_), channel_id=1, source_target_pairs={{0,1},{1,0},{2,3},{3,2},{4,5},{5,4},{6,7},{7,6},{8,9},{9,8},{10,11... | collective-permute-start | bytes 6152 | tf_op jit(solution)/shard_map/ppermute | solution.py:263

commit v2 on v1

--- a/solution.py
+++ b/solution.py
@@ -13,8 +13,7 @@
 RC = 128
 DC = 16
 NBINS = 256
-TILE = 32
-EXTRA = 32
+EXTRA = 16
 
 OPPONENT = ((0.2126, 0.7152, 0.0722), (0.5, -0.5, 0.0), (0.0, 0.4, -0.4))
 SPREAD = (0.6, 0.35, 0.35)
@@ -22,7 +21,6 @@
 
 F32 = jnp.float32
 BF16 = jnp.bfloat16
-VMEM_LIMIT = 48 * 1024 * 1024
 
 
 def iota(shape, dim):
@@ -49,23 +47,74 @@
     return table.reshape(NBINS, sample_num * DC).astype(ml_dtypes.bfloat16)
 
 
-def pack_kernel(visible, bins, ray_code, blend, truth, message):
+def pack_kernel(visible, bins, ray_code, blend, truth, message, names, lists, weights, truths, sems):
     pixels = ray_code.shape[0]
-    message[0:pixels] = ray_code[...]
-    lists = bins.shape[0] * bins.shape[1]
-    message[pixels : pixels + lists] = bins[...].astype(F32).reshape(lists, pixels).astype(BF16)
-    truths = truth[...].reshape(truth.shape[0], pixels)
-    rows = [visible[...].astype(F32)] + parts_of(blend[...]) + parts_of(truths)
+    listed = bins.shape[0] * bins.shape[1]
+    copies = [
+        pltpu.make_async_copy(source, target, sems.at[i])
+        for i, (source, target) in enumerate(
+            (
+                (ray_code, message.at[0:pixels]),
+                (bins, lists),
+                (visible, names),
+                (blend, weights),
+                (truth, truths),
+            )
+        )
+    ]
+    for copy in copies:
+        copy.start()
+    for copy in copies[1:]:
+        copy.wait()
+    message[pixels : pixels + listed] = lists[...].astype(F32).reshape(listed, pixels).astype(BF16)
+    shares = weights[...] / jnp.sum(weights[...], axis=0, keepdims=True)
+    rows = [names[...].astype(F32)] + parts_of(shares)
     used = sum(row.shape[0] for row in rows)
     rows.append(jnp.zeros((EXTRA - used, pixels), F32))
-    message[pixels + lists :] = jnp.concatenate(rows, axis=0).astype(BF16)
-
-
-def serve_kernel(sources, slots, *refs):
+    message[pixels + listed :] = jnp.concatenate(rows, axis=0).astype(BF16)
+    copies[0].wait()
+
+
+def tiles_for(most, large, small):
+    tiles = []
+    start = 0
+    while start < most:
+        for size in small + [large]:
+            low = small[small.index(size) - 1] if size in small[1:] else 0
+            if size == large:
+                low = small[-1]
+            if low < most - start:
+                high = start + size if size != large else most
+                tiles.append((start, size, start + low, high))
+        start += large
+    return tiles
+
+
+def prepare_kernel(samples, w_in, w_hid, w_out, first_w, hid_w, last_w, sem):
+    local_blocks, in_width, hidden = w_in.shape
+    load = pltpu.make_async_copy(w_hid, hid_w, sem)
+    load.start()
+    for k in range(local_blocks):
+        first_w[k, 0:RC] = w_in[k, 0:RC]
+        for i in range(RC // DC):
+            first_w[k, RC + i * DC : RC + (i + 1) * DC] = w_in[k, RC:]
+        wide = jnp.concatenate(
+            [
+                jnp.broadcast_to(w_out[k, c : c + 1].astype(F32), (samples, hidden))
+                for c in range(4)
+            ]
+            + [jnp.zeros((128 - 4 * samples, hidden), F32)],
+            axis=0,
+        )
+        last_w[k] = wide.T.astype(BF16)
+    load.wait()
+
+
+def serve_kernel(sources, slots, tiles, *refs):
     messages = refs[:sources]
-    w_in, w_hid, w_out, table, partial, aside = refs[sources : sources + 6]
-    places, mixed, codes, depths, first_w, last_w, heads = refs[sources + 6 :]
-    local_blocks, in_width, hidden = w_in.shape
+    truth, first_w, w_hid, last_w, table, partial = refs[sources : sources + 6]
+    places, mixed, codes, depths, heads = refs[sources + 6 :]
+    local_blocks = w_hid.shape[0]
     pixels = messages[0].shape[1]
     lists = messages[0].shape[0] - pixels - EXTRA
     samples = lists // 2
@@ -76,8 +125,10 @@
     named = []
     for s in range(sources):
         for v in range(2):
-            own = iota((8, pixels), 0) + first_block
-            hit = (extras[s][v : v + 1] == own.astype(F32)) & (iota((8, pixels), 0) < local_blocks)
+            block = iota((8, pixels), 0) + first_block
+            hit = (extras[s][v : v + 1] == block.astype(F32)) & (
+                iota((8, pixels), 0) < local_blocks
+            )
             named.append(hit.astype(F32))
     either = [named[2 * s] + named[2 * s + 1] for s in range(sources)]
     before = (iota((pixels, pixels), 0) < iota((pixels, pixels), 1)).astype(F32).astype(BF16)
@@ -96,10 +147,7 @@
                 places[k * slots : (k + 1) * slots, lanes] = (
                     (slot_row == spot[k : k + 1]).astype(F32).astype(BF16)
                 )
-    tiles = [
-        (jnp.max(offset[k : k + 1]).astype(jnp.int32) + TILE - 1) // TILE
-        for k in range(local_blocks)
-    ]
+    counts = [jnp.max(offset[k : k + 1]).astype(jnp.int32) for k in range(local_blocks)]
 
     lane = iota((pixels, pixels), 1)
     per_turn = pixels // lists
@@ -129,40 +177,34 @@
     heads[...] = jnp.zeros_like(heads)
     per_half = RC // DC
     for k in range(local_blocks):
-        first_w[0:RC] = w_in[k, 0:RC]
-        for i in range(per_half):
-            first_w[RC + i * DC : RC + (i + 1) * DC] = w_in[k, RC:]
-        wide = jnp.concatenate(
-            [jnp.broadcast_to(w_out[k, c : c + 1].astype(F32), (samples, hidden)) for c in range(4)]
-            + [jnp.zeros((128 - 4 * samples, hidden), F32)],
-            axis=0,
-        )
-        last_w[...] = wide.T.astype(BF16)
-
-        def one_tile(t, carry, k=k):
-            rows = pl.ds(pl.multiple_of(k * slots + t * TILE, TILE), TILE)
+
+        def one_tile(start, size, k=k):
+            rows = pl.ds(pl.multiple_of(k * slots + start, 16), size)
             code = codes[rows, :]
             depth = depths[rows, :]
-            half_lane = iota((TILE, RC), 1) // DC
+            half_lane = iota((size, RC), 1) // DC
             inputs = []
             for j in range(samples):
                 half = depth[:, (j // per_half) * RC : (j // per_half + 1) * RC]
                 kept = jnp.where(half_lane == j % per_half, half, jnp.zeros_like(half))
                 inputs.append(jnp.concatenate([code, kept], axis=1))
             inputs = jnp.concatenate(inputs, axis=0)
-            one = jnp.dot(inputs, first_w[...], preferred_element_type=F32)
+            one = jnp.dot(inputs, first_w[k], preferred_element_type=F32)
             one = jnp.maximum(one, 0.0).astype(BF16)
             two = jnp.dot(one, w_hid[k], preferred_element_type=F32)
             two = jnp.maximum(two, 0.0).astype(BF16)
-            out = jnp.dot(two, last_w[...], preferred_element_type=F32)
-            sample_lane = iota((TILE, 128), 1) % samples
-            total = jnp.zeros((TILE, 128), F32)
+            out = jnp.dot(two, last_w[k], preferred_element_type=F32)
+            sample_lane = iota((size, 128), 1) % samples
+            total = jnp.zeros((size, 128), F32)
             for j in range(samples):
-                total = jnp.where(sample_lane == j, out[j * TILE : (j + 1) * TILE], total)
+                total = jnp.where(sample_lane == j, out[j * size : (j + 1) * size], total)
             heads[rows, :] = total
-            return carry
-
-        lax.fori_loop(0, tiles[k], one_tile, 0)
+
+        for start, size, fewest, most in tiles:
+
+            @pl.when((counts[k] > fewest) & (counts[k] <= most))
+            def _(one_tile=one_tile, start=start, size=size):
+                one_tile(start, size)
 
     turned = heads[...].T
     optical = jax.nn.softplus(turned[0:samples]) * (1.5 / samples)
@@ -183,35 +225,30 @@
     stacked = jnp.concatenate(parts_of(shades) + [jnp.zeros_like(shades)], axis=0).astype(BF16)
     spots = jnp.dot(stacked, places[...], preferred_element_type=F32)
     spots = spots[0:4] + spots[4:8] + spots[8:12]
+    sums = []
     for s in range(sources):
-        blend = [extras[s][2 + v : 3 + v] + extras[s][4 + v : 5 + v] + extras[s][6 + v : 7 + v] for v in range(2)]
-        lanes = slice(s * pixels, (s + 1) * pixels)
-        mine = [spots[:, (2 * s + v) * pixels : (2 * s + v + 1) * pixels] * blend[v] for v in range(2)]
-        partial[:, lanes] = mine[0] + mine[1]
-        aside[0:3, lanes] = extras[s][8:11] + extras[s][11:14] + extras[s][14:17]
-        aside[3:4, lanes] = blend[0] + blend[1]
+        mine = []
+        for v in range(2):
+            share = extras[s][2 + v : 3 + v] + extras[s][4 + v : 5 + v] + extras[s][6 + v : 7 + v]
+            mine.append(spots[0:3, (2 * s + v) * pixels : (2 * s + v + 1) * pixels] * share)
+        sums.append(mine[0] + mine[1])
+    sums[0] = sums[0] - truth[...].reshape(3, pixels)
+    partial[...] = jnp.concatenate(sums, axis=0)
 
 
 def gather_kernel(sources, *refs):
     partials = refs[:sources]
-    aside, rendered, message = refs[sources:]
+    truth, rendered, message = refs[sources:]
     pixels = rendered.shape[2]
     z = lax.axis_index("block")
-
-    def block(ref, u):
-        return ref[:, u * pixels : (u + 1) * pixels]
-
     squared = jnp.zeros((3, pixels), F32)
     rows = []
     for u in range(sources):
-        total = block(partials[0], u)
+        difference = partials[0][3 * u : 3 * u + 3]
         for t in range(1, sources):
-            total = total + block(partials[t], t ^ u)
-        extra = block(aside, u)
-        shown = total[0:3] / extra[3:4]
+            difference = difference + partials[t][3 * (t ^ u) : 3 * (t ^ u) + 3]
         if u == 0:
-            rendered[...] = shown.reshape(3, 1, pixels)
-        difference = shown - extra[0:3]
+            rendered[...] = difference.reshape(3, 1, pixels) + truth[...]
         squared = squared + difference * difference
         rows.append(difference)
     above = jnp.zeros((3, pixels), F32)
@@ -219,13 +256,16 @@
     for u in range(1, sources):
         above = above + jnp.where((z ^ u) == z - 1, rows[u], 0.0)
         below = below + jnp.where((z ^ u) == z + 1, rows[u], 0.0)
-    for c in range(3):
-        def channel(d):
-            return sum(OPPONENT[c][i] * d[i : i + 1] for i in range(3) if OPPONENT[c][i])
-
-        message[c : c + 1] = SPREAD[c] * channel(above) + channel(rows[0]) + SPREAD[c] * channel(below)
+
+    def opponent(block, c):
+        return sum(OPPONENT[c][i] * block[i : i + 1] for i in range(3) if OPPONENT[c][i])
+
+    mixed = [
+        SPREAD[c] * opponent(above, c) + opponent(rows[0], c) + SPREAD[c] * opponent(below, c)
+        for c in range(3)
+    ]
     total = jnp.sum(jnp.sum(squared, axis=0, keepdims=True), axis=1, keepdims=True)
-    message[3:4] = jnp.broadcast_to(total, (1, pixels))
+    message[...] = jnp.concatenate(mixed + [jnp.broadcast_to(total, (1, pixels))], axis=0)
 
 
 def finish_kernel(columns, count, *refs):
@@ -249,8 +289,7 @@
     for c in range(3):
         column = SPREAD[c] * before[c : c + 1] + own[c : c + 1] + SPREAD[c] * after[c : c + 1]
         scale = np.float32(1.0) + np.float32(2.0) * np.float32(SPREAD[c])
-        filtered = column / float(scale * scale)
-        emphasised = EMPHASIS[c] * filtered
+        emphasised = EMPHASIS[c] * (column / float(scale * scale))
         summed = summed + emphasised * emphasised
     flip_map[...] = jnp.sqrt(summed + 1e-06)
     logged = jnp.log(total / count + 1e-06) * (-10.0 / math.log(10.0))
@@ -264,12 +303,19 @@
     return out
 
 
-def call(kernel, out_shape, scratch=(), flops=0, bytes_accessed=0):
+def call(
+    kernel, out_shape, in_specs, scratch, flops=0, bytes_accessed=0, limit=8 << 20
+):
+    cost = None
+    if flops:
+        cost = pl.CostEstimate(flops=flops, bytes_accessed=bytes_accessed, transcendentals=0)
     return pl.pallas_call(
         kernel,
         out_shape=out_shape,
+        in_specs=in_specs,
         scratch_shapes=list(scratch),
-        compiler_params=pltpu.CompilerParams(vmem_limit_bytes=VMEM_LIMIT),
+        cost_estimate=cost,
+        compiler_params=pltpu.CompilerParams(vmem_limit_bytes=limit),
     )
 
 
@@ -282,12 +328,23 @@
     samples = bins.shape[3]
     blocks_all = local_blocks * sources
     capacity = (2 * pixels * visible_num + blocks_all - 1) // blocks_all
-    slots = -(-sources * capacity // TILE) * TILE
-    slots_all = local_blocks * slots
     lists = visible_num * samples
     height = pixels + lists + EXTRA
-
-    message = call(pack_kernel, jax.ShapeDtypeStruct((height, pixels), BF16))(
+    far = pl.BlockSpec(memory_space=pltpu.HBM)
+    near = pl.BlockSpec(memory_space=pltpu.VMEM)
+    message = call(
+        pack_kernel,
+        jax.ShapeDtypeStruct((height, pixels), BF16),
+        [far] * 5,
+        (
+            pltpu.VMEM((visible_num, pixels), jnp.int32),
+            pltpu.VMEM((visible_num, samples, pixels), jnp.int32),
+            pltpu.VMEM((visible_num, pixels), F32),
+            pltpu.VMEM(truth.shape, F32),
+            pltpu.SemaphoreType.DMA((5,)),
+        ),
+        limit=64 << 20,
+    )(
         visible.reshape(pixels, visible_num).T,
         jnp.transpose(bins.reshape(pixels, visible_num, samples), (1, 2, 0)),
         ray_code.reshape(pixels, RC),
@@ -295,22 +352,39 @@
         truth,
     )
     messages = exchange(message, "block", sources)
-    partial, aside = call(
-        functools.partial(serve_kernel, sources, slots),
+    table = jnp.asarray(depth_table(samples))
+
+    slots = -(-sources * capacity // 16) * 16
+    tiles = tiles_for(slots, 96, [48, 80])
+    slots_all = local_blocks * slots
+    first_w, hid_w, last_w = call(
+        functools.partial(prepare_kernel, samples),
         (
-            jax.ShapeDtypeStruct((4, sources * pixels), F32),
-            jax.ShapeDtypeStruct((4, sources * pixels), F32),
-        ),
+            jax.ShapeDtypeStruct((local_blocks, 2 * RC, hidden), BF16),
+            jax.ShapeDtypeStruct(w_hid.shape, BF16),
+            jax.ShapeDtypeStruct((local_blocks, hidden, 128), BF16),
+        ),
+        [near, far, near],
+        (pltpu.SemaphoreType.DMA,),
+        limit=8 * 1024 * 1024,
+        flops=1 << 20,
+        bytes_accessed=1 << 22,
+    )(w_in, w_hid, w_out)
+    partial = call(
+        functools.partial(serve_kernel, sources, slots, tiles),
+        jax.ShapeDtypeStruct((3 * sources, pixels), F32),
+        [near] * (sources + 5),
         (
             pltpu.VMEM((slots_all, sources * visible_num * pixels), BF16),
             pltpu.VMEM((sources * visible_num * pixels, 2 * RC), BF16),
             pltpu.VMEM((slots_all, RC), BF16),
             pltpu.VMEM((slots_all, samples * DC), BF16),
-            pltpu.VMEM((2 * RC, hidden), BF16),
-            pltpu.VMEM((hidden, 128), BF16),
             pltpu.VMEM((-(-slots_all // 128) * 128, 128), F32),
         ),
-    )(*messages, w_in, w_hid, w_out, jnp.asarray(depth_table(samples)))
+        flops=2 * slots_all * samples * hidden * (in_width + hidden + 4),
+        bytes_accessed=2 * (w_in.size + w_hid.size),
+        limit=40 * 1024 * 1024,
+    )(*messages, truth, first_w, hid_w, last_w, table)
     partials = exchange(partial, "block", sources)
     rendered, edge = call(
         functools.partial(gather_kernel, sources),
@@ -318,7 +392,9 @@
             jax.ShapeDtypeStruct((3, 1, pixels), F32),
             jax.ShapeDtypeStruct((4, pixels), F32),
         ),
-    )(*partials, aside)
+        [near] * (sources + 1),
+        (),
+    )(*partials, truth)
     edges = exchange(edge, ("rep", "tile"), columns)
     flip_map, psnr = call(
         functools.partial(finish_kernel, columns, 3 * sources * columns * pixels),
@@ -326,6 +402,8 @@
             jax.ShapeDtypeStruct((1, pixels), F32),
             jax.ShapeDtypeStruct((1, 1), F32),
         ),
+        [near] * columns,
+        (),
     )(*edges)
     return (rendered, flip_map, psnr.reshape(1))
 

time: 42.2 us -> 34.6 us (0.82)
  Pallas kernels: 14.4 us -> 8.49 us
  local copies, waits for them, and re-layouts: 7.54 us -> 3.14 us
  starting transfers between devices: 12 us -> 15.9 us
  waiting for transfers between devices: 7.73 us -> 6.73 us
    pallas_call x2 -> x3, Pallas kernels: 13.2 us -> 7.29 us  [the longest x1 5.56 us: body(): call(functools.partial(serve_kernel, sources, slots, tiles), jax.ShapeDty...]
    unnamed x18 -> x12, local copies, waits for them, and re-layouts: 7.54 us -> 3.14 us
    ppermute x9, starting transfers between devices: 12 us -> 15.9 us  [exchange(): out.append(lax.ppermute(value, axes, [(i, i ^ s) for i in range(size)]))]
    ppermute x9, waiting for transfers between devices: 7.73 us -> 6.73 us  [exchange(): out.append(lax.ppermute(value, axes, [(i, i ^ s) for i in range(size)]))]
  transfers between devices with their start and end apart: 9 -> 9, of which waited for: 6 -> 5; matrix products, arithmetic and copies ran while one was open for 0% -> 0% of each run, Pallas kernels for 0% -> 1%
where the time goes in v2:
time: 34.6 us; the launch traced here: 35 us
  starting transfers between devices  15.9 us (46%)
  Pallas kernels  8.49 us (25%)
  waiting for transfers between devices  6.73 us (19%)
  local copies, waits for them, and re-layouts  3.14 us (9%)
  between operations  0.68 us (2%)
    ppermute x9, starting transfers between devices, exchange(): out.append(lax.ppermute(value, axes, [(i, i ^ s) for i in range(size)]))  15.9 us
    ppermute x9, waiting for transfers between devices, exchange(): out.append(lax.ppermute(value, axes, [(i, i ^ s) for i in range(size)]))  6.73 us
    pallas_call x1, Pallas kernels, body(): call(functools.partial(serve_kernel, sources, slots, tiles), jax.ShapeDty...  5.56 us
    unnamed x12, local copies, waits for them, and re-layouts  3.14 us
    pallas_call x1, Pallas kernels, body(): call(pack_kernel, jax.ShapeDtypeStruct((height, pixels), BF16), [far] * 5...  1.42 us
  transfers between devices with their start and end apart: 9, of which 5 were waited for; matrix products, arithmetic and copies ran while one was open for 0% of the time, Pallas kernels for 1%

profile of v2, /device:TPU:0, one launch (start us, length us, event | category | flops | bytes accessed | tf_op | source)
XLA Modules:
  0.0 35.0 jit_solution(16776315847332416203)
XLA Ops:
  0.6 1.4 %shard_map.112.refs_0_ = bf16[176,128]{1,0:T(8,128)(2,1)} custom-call(s32[2,128]{1,0:T(2,128)} %bitcast.13, s32[2,16,128]{2,1,0:T(8,128)} %bitcast.12, bf16[128,128]{1,0:T(8,128)(2,1)} %bitcast.11, f32[2,128]{1,0:T(2,128)} %bitcast.14, f32[3,1,128]{2,1,0:T(1,128)} %refs_4_.3), custom_call_target="tpu_custom_call" | custom-call | tf_op jit(solution)/shard_map/pallas_call | solution.py:335
  2.1 5.1 %collective-permute-start.2 = (bf16[176,128]{1,0:T(8,128)(2,1)}, bf16[176,128]{1,0:T(8,128)(2,1)S(1)}, u32[]{:S(2)}, u32[]{:S(2)}) collective-permute-start(bf16[176,128]{1,0:T(8,128)(2,1)} %shard_map.112.refs_0_), channel_id=1, source_target_pairs={{0,12},{4,8},{8,4},{12,0},{1,13},{5,9},{9,5},{13,1},{2,14},{6,10},... | collective-permute-start | bytes 135176 | tf_op jit(solution)/shard_map/ppermute | solution.py:302
  7.2 0.0 collective-permute-start.1
  7.2 0.6 %collective-permute-start = (bf16[176,128]{1,0:T(8,128)(2,1)}, bf16[176,128]{1,0:T(8,128)(2,1)S(1)}, u32[]{:S(2)}, u32[]{:S(2)}) collective-permute-start(bf16[176,128]{1,0:T(8,128)(2,1)} %shard_map.112.refs_0_), channel_id=1, source_target_pairs={{0,4},{4,0},{8,12},{12,8},{1,5},{5,1},{9,13},{13,9},{2,6},{6,2},{1... | collective-permute-start | bytes 135176 | tf_op jit(solution)/shard_map/ppermute | solution.py:302
  7.8 0.0 copy-start
  7.8 1.4 %copy-done = bf16[3,512,512]{2,1,0:T(8,128)(2,1)S(1)} copy-done((bf16[3,512,512]{2,1,0:T(8,128)(2,1)S(1)}, bf16[3,512,512]{2,1,0:T(8,128)(2,1)}, u32[]{:S(2)}) %copy-start) | copy-done | bytes 1572888
  9.2 0.0 copy-start.1
  9.2 1.0 %copy-done.1 = bf16[3,144,512]{2,1,0:T(8,128)(2,1)S(1)} copy-done((bf16[3,144,512]{2,1,0:T(8,128)(2,1)S(1)}, bf16[3,144,512]{2,1,0:T(8,128)(2,1)}, u32[]{:S(2)}) %copy-start.1) | copy-done | bytes 442392
  10.2 0.0 copy-start.3
  10.2 0.7 %copy-done.3 = bf16[3,4,512]{2,1,0:T(4,128)(2,1)S(1)} copy-done((bf16[3,4,512]{2,1,0:T(4,128)(2,1)S(1)}, bf16[3,4,512]{2,1,0:T(4,128)(2,1)}, u32[]{:S(2)}) %copy-start.3) | copy-done | bytes 12312
  10.9 0.0 copy-start.2
  11.0 0.0 copy-start.4
  11.0 0.0 copy-start.5
  11.0 0.3 shard_map.113
  11.3 0.0 collective-permute-done.2.refs_3_
  11.3 1.1 %collective-permute-done.1.refs_2_ = bf16[176,128]{1,0:T(8,128)(2,1)S(1)} collective-permute-done((bf16[176,128]{1,0:T(8,128)(2,1)}, bf16[176,128]{1,0:T(8,128)(2,1)S(1)}, u32[]{:S(2)}, u32[]{:S(2)}) %collective-permute-start.1) | collective-permute-done | bytes 45088 | tf_op jit(solution)/shard_map/ppermute | solution.py:302
  12.3 0.0 collective-permute-done.refs_1_
  12.3 0.0 copy-done.2
  12.3 0.0 copy-done.4
  12.3 0.0 copy-done.5
  12.4 5.6 %shard_map.114.refs_0_ = f32[12,128]{1,0:T(8,128)S(1)} custom-call(bf16[176,128]{1,0:T(8,128)(2,1)S(1)} %copy-done.2, bf16[176,128]{1,0:T(8,128)(2,1)S(1)} %collective-permute-done.refs_1_, bf16[176,128]{1,0:T(8,128)(2,1)S(1)} %collective-permute-done.1.refs_2_, bf16[176,128]{1,0:T(8,128)(2,1)S(1)} %collective-permute-done.2.refs_3_, ...), custom_call_target="tpu_custom_call" | custom-call | flops 5709496320 | bytes 2015232 | tf_op jit(solution)/shard_map/pallas_call | solution.py:373
  17.9 7.7 %collective-permute-start.5 = (f32[12,128]{1,0:T(8,128)S(1)}, f32[12,128]{1,0:T(8,128)S(1)}, u32[]{:S(2)}, u32[]{:S(2)}) collective-permute-start(f32[12,128]{1,0:T(8,128)S(1)} %shard_map.114.refs_0_), channel_id=1, source_target_pairs={{0,12},{4,8},{8,4},{12,0},{1,13},{5,9},{9,5},{13,1},{2,14},{6,10},... | collective-permute-start | bytes 18440 | tf_op jit(solution)/shard_map/ppermute | solution.py:302
  25.6 0.0 collective-permute-start.4
  25.6 0.6 %collective-permute-start.3 = (f32[12,128]{1,0:T(8,128)S(1)}, f32[12,128]{1,0:T(8,128)S(1)}, u32[]{:S(2)}, u32[]{:S(2)}) collective-permute-start(f32[12,128]{1,0:T(8,128)S(1)} %shard_map.114.refs_0_), channel_id=1, source_target_pairs={{0,4},{4,0},{8,12},{12,8},{1,5},{5,1},{9,13},{13,9},{2,6},{6,2},{1... | collective-permute-start | bytes 18440 | tf_op jit(solution)/shard_map/ppermute | solution.py:302
  26.2 1.0 %collective-permute-done.5.refs_3_ = f32[12,128]{1,0:T(8,128)S(1)} collective-permute-done((f32[12,128]{1,0:T(8,128)S(1)}, f32[12,128]{1,0:T(8,128)S(1)}, u32[]{:S(2)}, u32[]{:S(2)}) %collective-permute-start.5) | collective-permute-done | bytes 6176 | tf_op jit(solution)/shard_map/ppermute | solution.py:302
  27.2 2.9 %collective-permute-done.4.refs_2_ = f32[12,128]{1,0:T(8,128)S(1)} collective-permute-done((f32[12,128]{1,0:T(8,128)S(1)}, f32[12,128]{1,0:T(8,128)S(1)}, u32[]{:S(2)}, u32[]{:S(2)}) %collective-permute-start.4) | collective-permute-done | bytes 6176 | tf_op jit(solution)/shard_map/ppermute | solution.py:302
  30.1 0.0 collective-permute-done.3.refs_1_
  30.1 0.6 %shard_map.115 = (f32[3,1,128]{2,1,0:T(1,128)}, f32[4,128]{1,0:T(4,128)S(1)}) custom-call(f32[12,128]{1,0:T(8,128)S(1)} %shard_map.114.refs_0_, f32[12,128]{1,0:T(8,128)S(1)} %collective-permute-done.3.refs_1_, f32[12,128]{1,0:T(8,128)S(1)} %collective-permute-done.4.refs_2_, f32[12,128]{1,0:T(8,128)S(1)} %collective-permute-done.5.refs_3_, ...), custom_call_target="tpu_custom_call" | custom-call | tf_op jit(solution)/shard_map/pallas_call | solution.py:389
  30.7 0.0 collective-permute-start.8
  30.7 1.5 %collective-permute-start.7 = (f32[4,128]{1,0:T(4,128)S(1)}, f32[4,128]{1,0:T(4,128)S(1)}, u32[]{:S(2)}, u32[]{:S(2)}) collective-permute-start(f32[4,128]{1,0:T(4,128)S(1)} %get-tuple-element.14.refs_0_), channel_id=1, source_target_pairs={{0,2},{1,3},{2,0},{3,1},{4,6},{5,7},{6,4},{7,5},{8,10},{9,11},{10,... | collective-permute-start | bytes 6152 | tf_op jit(solution)/shard_map/ppermute | solution.py:302
  32.3 0.3 collective-permute-start.6
  32.6 1.1 %collective-permute-done.8.refs_3_ = f32[4,128]{1,0:T(4,128)S(1)} collective-permute-done((f32[4,128]{1,0:T(4,128)S(1)}, f32[4,128]{1,0:T(4,128)S(1)}, u32[]{:S(2)}, u32[]{:S(2)}) %collective-permute-start.8) | collective-permute-done | bytes 2080 | tf_op jit(solution)/shard_map/ppermute | solution.py:302
  33.7 0.6 %collective-permute-done.7.refs_2_ = f32[4,128]{1,0:T(4,128)S(1)} collective-permute-done((f32[4,128]{1,0:T(4,128)S(1)}, f32[4,128]{1,0:T(4,128)S(1)}, u32[]{:S(2)}, u32[]{:S(2)}) %collective-permute-start.7) | collective-permute-done | bytes 2080 | tf_op jit(solution)/shard_map/ppermute | solution.py:302
  34.3 0.0 collective-permute-done.6.refs_1_
  34.3 0.6 %shard_map.116 = (f32[1,128]{1,0:T(1,128)}, f32[1,1]{1,0:T(1,128)}) custom-call(f32[4,128]{1,0:T(4,128)S(1)} %get-tuple-element.14.refs_0_, f32[4,128]{1,0:T(4,128)S(1)} %collective-permute-done.6.refs_1_, f32[4,128]{1,0:T(4,128)S(1)} %collective-permute-done.7.refs_2_, f32[4,128]{1,0:T(4,128)S(1)} %collective-permute-done.8.refs_3_), custom_call_target="tpu_custom_call" | custom-call | tf_op jit(solution)/shard_map/pallas_call | solution.py:399
Async XLA Ops:
  2.1 9.2 %collective-permute-start.2 = (bf16[176,128]{1,0:T(8,128)(2,1)}, bf16[176,128]{1,0:T(8,128)(2,1)S(1)}, u32[]{:S(2)}, u32[]{:S(2)}) collective-permute-start(bf16[176,128]{1,0:T(8,128)(2,1)} %shard_map.112.refs_0_), channel_id=1, source_target_pairs={{0,12},{4,8},{8,4},{12,0},{1,13},{5,9},{9,5},{13,1},{2,14},{6,10},... | collective-permute-start | bytes 135176 | tf_op jit(solution)/shard_map/ppermute | solution.py:302
  7.2 5.2 %collective-permute-start.1 = (bf16[176,128]{1,0:T(8,128)(2,1)}, bf16[176,128]{1,0:T(8,128)(2,1)S(1)}, u32[]{:S(2)}, u32[]{:S(2)}) collective-permute-start(bf16[176,128]{1,0:T(8,128)(2,1)} %shard_map.112.refs_0_), channel_id=1, source_target_pairs={{0,8},{4,12},{8,0},{12,4},{1,9},{5,13},{9,1},{13,5},{2,10},{6,14},... | collective-permute-start | bytes 135176 | tf_op jit(solution)/shard_map/ppermute | solution.py:302
  7.2 5.2 %collective-permute-start = (bf16[176,128]{1,0:T(8,128)(2,1)}, bf16[176,128]{1,0:T(8,128)(2,1)S(1)}, u32[]{:S(2)}, u32[]{:S(2)}) collective-permute-start(bf16[176,128]{1,0:T(8,128)(2,1)} %shard_map.112.refs_0_), channel_id=1, source_target_pairs={{0,4},{4,0},{8,12},{12,8},{1,5},{5,1},{9,13},{13,9},{2,6},{6,2},{1... | collective-permute-start | bytes 135176 | tf_op jit(solution)/shard_map/ppermute | solution.py:302
  7.8 1.4 %copy-start = (bf16[3,512,512]{2,1,0:T(8,128)(2,1)S(1)}, bf16[3,512,512]{2,1,0:T(8,128)(2,1)}, u32[]{:S(2)}) copy-start(bf16[3,512,512]{2,1,0:T(8,128)(2,1)} %w_hid.1) | copy-start | bytes 4718596
  9.2 1.0 %copy-start.1 = (bf16[3,144,512]{2,1,0:T(8,128)(2,1)S(1)}, bf16[3,144,512]{2,1,0:T(8,128)(2,1)}, u32[]{:S(2)}) copy-start(bf16[3,144,512]{2,1,0:T(8,128)(2,1)} %w_in.1) | copy-start | bytes 1327108
  10.2 0.7 %copy-start.3 = (bf16[3,4,512]{2,1,0:T(4,128)(2,1)S(1)}, bf16[3,4,512]{2,1,0:T(4,128)(2,1)}, u32[]{:S(2)}) copy-start(bf16[3,4,512]{2,1,0:T(4,128)(2,1)} %w_out.1) | copy-start | bytes 36868
  10.9 1.4 %copy-start.2 = (bf16[176,128]{1,0:T(8,128)(2,1)S(1)}, bf16[176,128]{1,0:T(8,128)(2,1)}, u32[]{:S(2)}) copy-start(bf16[176,128]{1,0:T(8,128)(2,1)} %shard_map.112.refs_0_) | copy-start | bytes 135172
  11.0 1.4 %copy-start.4 = (f32[3,1,128]{2,1,0:T(1,128)S(1)}, f32[3,1,128]{2,1,0:T(1,128)}, u32[]{:S(2)}) copy-start(f32[3,1,128]{2,1,0:T(1,128)} %refs_4_.3) | copy-start | bytes 4612
  11.0 1.4 %copy-start.5 = (bf16[256,256]{1,0:T(8,128)(2,1)S(1)}, bf16[256,256]{1,0:T(8,128)(2,1)}, u32[]{:S(2)}) copy-start(bf16[256,256]{1,0:T(8,128)(2,1)} %constant.2.clone.refs_8_) | copy-start | bytes 393220
  17.9 9.3 %collective-permute-start.5 = (f32[12,128]{1,0:T(8,128)S(1)}, f32[12,128]{1,0:T(8,128)S(1)}, u32[]{:S(2)}, u32[]{:S(2)}) collective-permute-start(f32[12,128]{1,0:T(8,128)S(1)} %shard_map.114.refs_0_), channel_id=1, source_target_pairs={{0,12},{4,8},{8,4},{12,0},{1,13},{5,9},{9,5},{13,1},{2,14},{6,10},... | collective-permute-start | bytes 18440 | tf_op jit(solution)/shard_map/ppermute | solution.py:302
  25.6 4.5 %collective-permute-start.4 = (f32[12,128]{1,0:T(8,128)S(1)}, f32[12,128]{1,0:T(8,128)S(1)}, u32[]{:S(2)}, u32[]{:S(2)}) collective-permute-start(f32[12,128]{1,0:T(8,128)S(1)} %shard_map.114.refs_0_), channel_id=1, source_target_pairs={{0,8},{4,12},{8,0},{12,4},{1,9},{5,13},{9,1},{13,5},{2,10},{6,14},... | collective-permute-start | bytes 18440 | tf_op jit(solution)/shard_map/ppermute | solution.py:302
  25.6 4.5 %collective-permute-start.3 = (f32[12,128]{1,0:T(8,128)S(1)}, f32[12,128]{1,0:T(8,128)S(1)}, u32[]{:S(2)}, u32[]{:S(2)}) collective-permute-start(f32[12,128]{1,0:T(8,128)S(1)} %shard_map.114.refs_0_), channel_id=1, source_target_pairs={{0,4},{4,0},{8,12},{12,8},{1,5},{5,1},{9,13},{13,9},{2,6},{6,2},{1... | collective-permute-start | bytes 18440 | tf_op jit(solution)/shard_map/ppermute | solution.py:302
  30.7 3.0 %collective-permute-start.8 = (f32[4,128]{1,0:T(4,128)S(1)}, f32[4,128]{1,0:T(4,128)S(1)}, u32[]{:S(2)}, u32[]{:S(2)}) collective-permute-start(f32[4,128]{1,0:T(4,128)S(1)} %get-tuple-element.14.refs_0_), channel_id=1, source_target_pairs={{0,3},{1,2},{2,1},{3,0},{4,7},{5,6},{6,5},{7,4},{8,11},{9,10},{10,... | collective-permute-start | bytes 6152 | tf_op jit(solution)/shard_map/ppermute | solution.py:302
  30.7 3.6 %collective-permute-start.7 = (f32[4,128]{1,0:T(4,128)S(1)}, f32[4,128]{1,0:T(4,128)S(1)}, u32[]{:S(2)}, u32[]{:S(2)}) collective-permute-start(f32[4,128]{1,0:T(4,128)S(1)} %get-tuple-element.14.refs_0_), channel_id=1, source_target_pairs={{0,2},{1,3},{2,0},{3,1},{4,6},{5,7},{6,4},{7,5},{8,10},{9,11},{10,... | collective-permute-start | bytes 6152 | tf_op jit(solution)/shard_map/ppermute | solution.py:302
  32.3 2.1 %collective-permute-start.6 = (f32[4,128]{1,0:T(4,128)S(1)}, f32[4,128]{1,0:T(4,128)S(1)}, u32[]{:S(2)}, u32[]{:S(2)}) collective-permute-start(f32[4,128]{1,0:T(4,128)S(1)} %get-tuple-element.14.refs_0_), channel_id=1, source_target_pairs={{0,1},{1,0},{2,3},{3,2},{4,5},{5,4},{6,7},{7,6},{8,9},{9,8},{10,11... | collective-permute-start | bytes 6152 | tf_op jit(solution)/shard_map/ppermute | solution.py:302

commit v3 on v2

--- a/solution.py
+++ b/solution.py
@@ -47,47 +47,29 @@
     return table.reshape(NBINS, sample_num * DC).astype(ml_dtypes.bfloat16)
 
 
-def pack_kernel(visible, bins, ray_code, blend, truth, message, names, lists, weights, truths, sems):
+def blank_kernel(rows):
+    rows[...] = jnp.zeros_like(rows)
+
+
+def pack_kernel(visible, bins, ray_code, blend, blank, message):
     pixels = ray_code.shape[0]
     listed = bins.shape[0] * bins.shape[1]
-    copies = [
-        pltpu.make_async_copy(source, target, sems.at[i])
-        for i, (source, target) in enumerate(
-            (
-                (ray_code, message.at[0:pixels]),
-                (bins, lists),
-                (visible, names),
-                (blend, weights),
-                (truth, truths),
-            )
-        )
-    ]
-    for copy in copies:
-        copy.start()
-    for copy in copies[1:]:
-        copy.wait()
-    message[pixels : pixels + listed] = lists[...].astype(F32).reshape(listed, pixels).astype(BF16)
-    shares = weights[...] / jnp.sum(weights[...], axis=0, keepdims=True)
-    rows = [names[...].astype(F32)] + parts_of(shares)
-    used = sum(row.shape[0] for row in rows)
-    rows.append(jnp.zeros((EXTRA - used, pixels), F32))
+    message[0:pixels] = ray_code[...]
+    message[pixels : pixels + listed] = bins[...].astype(F32).reshape(listed, pixels).astype(BF16)
+    shares = blend[...] / jnp.sum(blend[...], axis=0, keepdims=True)
+    rows = [visible[...].astype(F32)] + parts_of(shares) + [blank[...]]
     message[pixels + listed :] = jnp.concatenate(rows, axis=0).astype(BF16)
-    copies[0].wait()
-
-
-def tiles_for(most, large, small):
-    tiles = []
-    start = 0
-    while start < most:
-        for size in small + [large]:
-            low = small[small.index(size) - 1] if size in small[1:] else 0
-            if size == large:
-                low = small[-1]
-            if low < most - start:
-                high = start + size if size != large else most
-                tiles.append((start, size, start + low, high))
-        start += large
-    return tiles
+
+
+def tiles_for(most, sizes):
+    bounds = [0] + [size for size in sizes if size < most] + [most]
+    return [(high, low, high) for low, high in zip(bounds, bounds[1:])]
+
+
+def layout_kernel(samples, before, spread):
+    before[...] = (iota(before.shape, 0) < iota(before.shape, 1)).astype(F32).astype(BF16)
+    here = iota(spread.shape, 0) % samples == iota(spread.shape, 1) // DC
+    spread[...] = here.astype(F32).astype(BF16)
 
 
 def prepare_kernel(samples, w_in, w_hid, w_out, first_w, hid_w, last_w, sem):
@@ -112,8 +94,8 @@
 
 def serve_kernel(sources, slots, tiles, *refs):
     messages = refs[:sources]
-    truth, first_w, w_hid, last_w, table, partial = refs[sources : sources + 6]
-    places, mixed, codes, depths, heads = refs[sources + 6 :]
+    truth, first_w, w_hid, last_w, table, before, spread, partial = refs[sources : sources + 8]
+    places, mixed, codes, depths, heads = refs[sources + 8 :]
     local_blocks = w_hid.shape[0]
     pixels = messages[0].shape[1]
     lists = messages[0].shape[0] - pixels - EXTRA
@@ -131,9 +113,8 @@
             )
             named.append(hit.astype(F32))
     either = [named[2 * s] + named[2 * s + 1] for s in range(sources)]
-    before = (iota((pixels, pixels), 0) < iota((pixels, pixels), 1)).astype(F32).astype(BF16)
     ranks = jnp.dot(
-        jnp.concatenate(either, axis=0).astype(BF16), before, preferred_element_type=F32
+        jnp.concatenate(either, axis=0).astype(BF16), before[...], preferred_element_type=F32
     )
     offset = jnp.zeros((8, 1), F32)
     slot_row = iota((slots, pixels), 0).astype(F32)
@@ -168,17 +149,18 @@
 
     chosen = jnp.dot(places[...], mixed[...], preferred_element_type=F32).astype(BF16)
     codes[...] = chosen[:, :RC]
-    spread_shape = (pixels, samples * DC)
-    spread = (iota(spread_shape, 0) % samples == iota(spread_shape, 1) // DC).astype(F32)
-    bins = jnp.dot(chosen[:, RC:], spread.astype(BF16), preferred_element_type=F32)
+    bins = jnp.dot(chosen[:, RC:], spread[...], preferred_element_type=F32)
     is_bin = (bins == iota(bins.shape, 1).astype(F32)).astype(F32).astype(BF16)
     depths[...] = jnp.dot(is_bin, table[...], preferred_element_type=F32).astype(BF16)
 
     heads[...] = jnp.zeros_like(heads)
     per_half = RC // DC
-    for k in range(local_blocks):
-
-        def one_tile(start, size, k=k):
+    def one_block(k, carry):
+        count = carry[0]
+        for i in range(1, local_blocks):
+            count = jnp.where(k == i, carry[i], count)
+
+        def one_tile(start, size):
             rows = pl.ds(pl.multiple_of(k * slots + start, 16), size)
             code = codes[rows, :]
             depth = depths[rows, :]
@@ -200,11 +182,15 @@
                 total = jnp.where(sample_lane == j, out[j * size : (j + 1) * size], total)
             heads[rows, :] = total
 
-        for start, size, fewest, most in tiles:
-
-            @pl.when((counts[k] > fewest) & (counts[k] <= most))
-            def _(one_tile=one_tile, start=start, size=size):
-                one_tile(start, size)
+        for size, fewest, most in tiles:
+
+            @pl.when((count > fewest) & (count <= most))
+            def _(size=size):
+                one_tile(0, size)
+
+        return carry
+
+    lax.fori_loop(0, local_blocks, one_block, tuple(counts))
 
     turned = heads[...].T
     optical = jax.nn.softplus(turned[0:samples]) * (1.5 / samples)
@@ -238,8 +224,8 @@
 
 def gather_kernel(sources, *refs):
     partials = refs[:sources]
-    truth, rendered, message = refs[sources:]
-    pixels = rendered.shape[2]
+    (message,) = refs[sources:]
+    pixels = message.shape[1]
     z = lax.axis_index("block")
     squared = jnp.zeros((3, pixels), F32)
     rows = []
@@ -247,8 +233,6 @@
         difference = partials[0][3 * u : 3 * u + 3]
         for t in range(1, sources):
             difference = difference + partials[t][3 * (t ^ u) : 3 * (t ^ u) + 3]
-        if u == 0:
-            rendered[...] = difference.reshape(3, 1, pixels) + truth[...]
         squared = squared + difference * difference
         rows.append(difference)
     above = jnp.zeros((3, pixels), F32)
@@ -265,20 +249,23 @@
         for c in range(3)
     ]
     total = jnp.sum(jnp.sum(squared, axis=0, keepdims=True), axis=1, keepdims=True)
-    message[...] = jnp.concatenate(mixed + [jnp.broadcast_to(total, (1, pixels))], axis=0)
+    message[...] = jnp.concatenate(
+        mixed + [jnp.broadcast_to(total, (1, pixels)), rows[0]], axis=0
+    )
 
 
 def finish_kernel(columns, count, *refs):
     messages = refs[:columns]
-    flip_map, psnr = refs[columns:]
+    truth, rendered, flip_map, psnr = refs[columns:]
     pixels = flip_map.shape[1]
     q = lax.axis_index("rep") * lax.axis_size("tile") + lax.axis_index("tile")
-    own = messages[0][...]
+    rendered[...] = messages[0][4:7].reshape(3, 1, pixels) + truth[...]
+    own = messages[0][0:4]
     left = jnp.zeros_like(own)
     right = jnp.zeros_like(own)
     total = own[3:4]
     for s in range(1, columns):
-        other = messages[s][...]
+        other = messages[s][0:4]
         left = left + jnp.where((q ^ s) == q - 1, other, 0.0)
         right = right + jnp.where((q ^ s) == q + 1, other, 0.0)
         total = total + other[3:4]
@@ -332,31 +319,41 @@
     height = pixels + lists + EXTRA
     far = pl.BlockSpec(memory_space=pltpu.HBM)
     near = pl.BlockSpec(memory_space=pltpu.VMEM)
+    blank = call(
+        blank_kernel,
+        jax.ShapeDtypeStruct((EXTRA - 4 * visible_num, pixels), F32),
+        [],
+        (),
+        flops=1 << 32,
+        bytes_accessed=1 << 17,
+    )()
     message = call(
-        pack_kernel,
-        jax.ShapeDtypeStruct((height, pixels), BF16),
-        [far] * 5,
-        (
-            pltpu.VMEM((visible_num, pixels), jnp.int32),
-            pltpu.VMEM((visible_num, samples, pixels), jnp.int32),
-            pltpu.VMEM((visible_num, pixels), F32),
-            pltpu.VMEM(truth.shape, F32),
-            pltpu.SemaphoreType.DMA((5,)),
-        ),
-        limit=64 << 20,
+        pack_kernel, jax.ShapeDtypeStruct((height, pixels), BF16), [near] * 5, ()
     )(
         visible.reshape(pixels, visible_num).T,
         jnp.transpose(bins.reshape(pixels, visible_num, samples), (1, 2, 0)),
         ray_code.reshape(pixels, RC),
         blend.reshape(pixels, visible_num).T,
-        truth,
+        blank,
     )
     messages = exchange(message, "block", sources)
     table = jnp.asarray(depth_table(samples))
 
     slots = -(-sources * capacity // 16) * 16
-    tiles = tiles_for(slots, 96, [48, 80])
+    tiles = tiles_for(slots, list(range(16, slots, 16)))
     slots_all = local_blocks * slots
+    before, spread = call(
+        functools.partial(layout_kernel, samples),
+        (
+            jax.ShapeDtypeStruct((pixels, pixels), BF16),
+            jax.ShapeDtypeStruct((pixels, samples * DC), BF16),
+        ),
+        [],
+        (),
+        limit=8 * 1024 * 1024,
+        flops=1 << 32,
+        bytes_accessed=1 << 17,
+    )()
     first_w, hid_w, last_w = call(
         functools.partial(prepare_kernel, samples),
         (
@@ -373,7 +370,7 @@
     partial = call(
         functools.partial(serve_kernel, sources, slots, tiles),
         jax.ShapeDtypeStruct((3 * sources, pixels), F32),
-        [near] * (sources + 5),
+        [near] * (sources + 7),
         (
             pltpu.VMEM((slots_all, sources * visible_num * pixels), BF16),
             pltpu.VMEM((sources * visible_num * pixels, 2 * RC), BF16),
@@ -384,27 +381,25 @@
         flops=2 * slots_all * samples * hidden * (in_width + hidden + 4),
         bytes_accessed=2 * (w_in.size + w_hid.size),
         limit=40 * 1024 * 1024,
-    )(*messages, truth, first_w, hid_w, last_w, table)
+    )(*messages, truth, first_w, hid_w, last_w, table, before, spread)
     partials = exchange(partial, "block", sources)
-    rendered, edge = call(
+    edge = call(
         functools.partial(gather_kernel, sources),
+        jax.ShapeDtypeStruct((7, pixels), F32),
+        [near] * sources,
+        (),
+    )(*partials)
+    edges = exchange(edge, ("rep", "tile"), columns)
+    rendered, flip_map, psnr = call(
+        functools.partial(finish_kernel, columns, 3 * sources * columns * pixels),
         (
             jax.ShapeDtypeStruct((3, 1, pixels), F32),
-            jax.ShapeDtypeStruct((4, pixels), F32),
-        ),
-        [near] * (sources + 1),
-        (),
-    )(*partials, truth)
-    edges = exchange(edge, ("rep", "tile"), columns)
-    flip_map, psnr = call(
-        functools.partial(finish_kernel, columns, 3 * sources * columns * pixels),
-        (
             jax.ShapeDtypeStruct((1, pixels), F32),
             jax.ShapeDtypeStruct((1, 1), F32),
         ),
-        [near] * columns,
+        [near] * (columns + 1),
         (),
-    )(*edges)
+    )(*edges, truth)
     return (rendered, flip_map, psnr.reshape(1))
 
 

time: 34.6 us -> 30.9 us (0.89); the launches traced: 35 us -> 30.7 us
  starting transfers between devices: 15.9 us -> 12.1 us
  local copies, waits for them, and re-layouts: 3.14 us -> 0.77 us
  waiting for transfers between devices: 6.73 us -> 8.86 us
    ppermute x9, starting transfers between devices: 15.9 us -> 12.1 us  [exchange(): out.append(lax.ppermute(value, axes, [(i, i ^ s) for i in range(size)]))]
    unnamed x12 -> x18, local copies, waits for them, and re-layouts: 3.14 us -> 0.77 us
    ppermute x9, waiting for transfers between devices: 6.73 us -> 8.86 us  [exchange(): out.append(lax.ppermute(value, axes, [(i, i ^ s) for i in range(size)]))]
    pallas_call x2 -> x4, Pallas kernels: 2.01 us -> 0.14 us  [the longest x1 0.09 us: body(): call(functools.partial(gather_kernel, sources), jax.ShapeDtypeStruct((7,...]
    pallas_call x1, Pallas kernels: 5.56 us -> 7.14 us  [body(): call(functools.partial(serve_kernel, sources, slots, tiles), jax.ShapeDty...]
  transfers between devices with their start and end apart: 9 -> 9, of which waited for: 5 -> 6; matrix products, arithmetic and copies ran while one was open for 0% -> 0% of each run, Pallas kernels for 1% -> 1%
where the time goes in v3:
time: 30.9 us; the launch traced here: 30.7 us
  starting transfers between devices  12.1 us (39%)
  waiting for transfers between devices  8.86 us (29%)
  Pallas kernels  8.21 us (27%)
  local copies, waits for them, and re-layouts  0.77 us (2%)
  between operations  0.77 us (2%)
    ppermute x9, starting transfers between devices, exchange(): out.append(lax.ppermute(value, axes, [(i, i ^ s) for i in range(size)]))  12.1 us
    ppermute x9, waiting for transfers between devices, exchange(): out.append(lax.ppermute(value, axes, [(i, i ^ s) for i in range(size)]))  8.86 us
    pallas_call x1, Pallas kernels, body(): call(functools.partial(serve_kernel, sources, slots, tiles), jax.ShapeDty...  7.14 us
    unnamed x18, local copies, waits for them, and re-layouts  0.77 us
    pallas_call x1, Pallas kernels, body(): call(functools.partial(finish_kernel, columns, 3 * sources * columns * pi...  0.62 us
  transfers between devices with their start and end apart: 9, of which 6 were waited for; matrix products, arithmetic and copies ran while one was open for 0% of the time, Pallas kernels for 1%

profile of v3, /device:TPU:0, one launch (start us, length us, event | category | flops | bytes accessed | tf_op | source)
XLA Modules:
  0.0 30.7 jit_solution(9681902451177544606)
XLA Ops:
  0.6 0.0 copy-start.7
  0.6 0.0 copy-start.2
  0.7 0.0 copy-start.3
  0.7 0.0 copy-start.6
  0.7 0.6 %copy-done.7 = f32[1,128,2]{1,2,0:T(2,128)S(1)} copy-done((f32[1,128,2]{1,2,0:T(2,128)S(1)}, f32[1,128,2]{1,2,0:T(2,128)}, u32[]{:S(2)}) %copy-start.7) | copy-done | bytes 1048
  1.3 0.1 copy-done.2
  1.4 0.0 copy-done.3
  1.4 0.0 copy-done.6
  1.4 0.0 copy-start
  1.4 0.0 copy-start.1
  1.5 0.0 copy-start.4
  1.5 5.1 %collective-permute-start.2 = (bf16[176,128]{1,0:T(8,128)(2,1)S(1)}, bf16[176,128]{1,0:T(8,128)(2,1)S(1)}, u32[]{:S(2)}, u32[]{:S(2)}) collective-permute-start(bf16[176,128]{1,0:T(8,128)(2,1)S(1)} %shard_map.113.refs_0_), channel_id=1, source_target_pairs={{0,12},{4,8},{8,4},{12,0},{1,13},{5,9},{9,5},{13,1},{2,14},{6,10},... | collective-permute-start | bytes 135176 | tf_op jit(solution)/shard_map/ppermute | solution.py:289
  6.6 0.0 collective-permute-start.1
  6.6 0.6 %collective-permute-start = (bf16[176,128]{1,0:T(8,128)(2,1)S(1)}, bf16[176,128]{1,0:T(8,128)(2,1)S(1)}, u32[]{:S(2)}, u32[]{:S(2)}) collective-permute-start(bf16[176,128]{1,0:T(8,128)(2,1)S(1)} %shard_map.113.refs_0_), channel_id=1, source_target_pairs={{0,4},{4,0},{8,12},{12,8},{1,5},{5,1},{9,13},{13,9},{2,6},{6,2},{1... | collective-permute-start | bytes 135176 | tf_op jit(solution)/shard_map/ppermute | solution.py:289
  7.3 0.0 copy-done
  7.3 0.0 copy-done.1
  7.3 0.0 copy-done.4
  7.3 0.0 copy-start.5
  7.3 0.0 copy-start.8
  7.3 0.3 %shard_map.114 = (bf16[3,256,512]{2,1,0:T(8,128)(2,1)S(1)}, bf16[3,512,512]{2,1,0:T(8,128)(2,1)S(1)}, bf16[3,512,128]{2,1,0:T(8,128)(2,1)S(1)}) custom-call(bf16[3,144,512]{2,1,0:T(8,128)(2,1)S(1)} %copy-done.1, bf16[3,512,512]{2,1,0:T(8,128)(2,1)S(1)} %copy-done, bf16[3,4,512]{2,1,0:T(4,128)(2,1)S(1)} %copy-done.4), custom_call_target="tpu_custom_call" | custom-call | flops 1048576 | bytes 4194304 | tf_op jit(solution)/shard_map/pallas_call | solution.py:357
  7.6 1.0 %collective-permute-done.2.refs_3_ = bf16[176,128]{1,0:T(8,128)(2,1)S(1)} collective-permute-done((bf16[176,128]{1,0:T(8,128)(2,1)S(1)}, bf16[176,128]{1,0:T(8,128)(2,1)S(1)}, u32[]{:S(2)}, u32[]{:S(2)}) %collective-permute-start.2) | collective-permute-done | bytes 45088 | tf_op jit(solution)/shard_map/ppermute | solution.py:289
  8.7 2.9 %collective-permute-done.1.refs_2_ = bf16[176,128]{1,0:T(8,128)(2,1)S(1)} collective-permute-done((bf16[176,128]{1,0:T(8,128)(2,1)S(1)}, bf16[176,128]{1,0:T(8,128)(2,1)S(1)}, u32[]{:S(2)}, u32[]{:S(2)}) %collective-permute-start.1) | collective-permute-done | bytes 45088 | tf_op jit(solution)/shard_map/ppermute | solution.py:289
  11.5 0.0 collective-permute-done.refs_1_
  11.5 0.0 copy-done.5
  11.5 0.0 copy-done.8
  11.5 7.1 %shard_map.116.refs_0_ = f32[12,128]{1,0:T(8,128)S(1)} custom-call(bf16[176,128]{1,0:T(8,128)(2,1)S(1)} %shard_map.113.refs_0_, bf16[176,128]{1,0:T(8,128)(2,1)S(1)} %collective-permute-done.refs_1_, bf16[176,128]{1,0:T(8,128)(2,1)S(1)} %collective-permute-done.1.refs_2_, bf16[176,128]{1,0:T(8,128)(2,1)S(1)} %collective-permute-done.2.refs_3_, ...), custom_call_target="tpu_custom_call" | custom-call | flops 5709496320 | bytes 2015232 | tf_op jit(solution)/shard_map/pallas_call | solution.py:370
  18.7 3.0 %collective-permute-start.5 = (f32[12,128]{1,0:T(8,128)S(1)}, f32[12,128]{1,0:T(8,128)S(1)}, u32[]{:S(2)}, u32[]{:S(2)}) collective-permute-start(f32[12,128]{1,0:T(8,128)S(1)} %shard_map.116.refs_0_), channel_id=1, source_target_pairs={{0,12},{4,8},{8,4},{12,0},{1,13},{5,9},{9,5},{13,1},{2,14},{6,10},... | collective-permute-start | bytes 18440 | tf_op jit(solution)/shard_map/ppermute | solution.py:289
  21.7 0.0 collective-permute-start.4
  21.7 1.4 %collective-permute-start.3 = (f32[12,128]{1,0:T(8,128)S(1)}, f32[12,128]{1,0:T(8,128)S(1)}, u32[]{:S(2)}, u32[]{:S(2)}) collective-permute-start(f32[12,128]{1,0:T(8,128)S(1)} %shard_map.116.refs_0_), channel_id=1, source_target_pairs={{0,4},{4,0},{8,12},{12,8},{1,5},{5,1},{9,13},{13,9},{2,6},{6,2},{1... | collective-permute-start | bytes 18440 | tf_op jit(solution)/shard_map/ppermute | solution.py:289
  23.1 1.1 %collective-permute-done.5.refs_3_ = f32[12,128]{1,0:T(8,128)S(1)} collective-permute-done((f32[12,128]{1,0:T(8,128)S(1)}, f32[12,128]{1,0:T(8,128)S(1)}, u32[]{:S(2)}, u32[]{:S(2)}) %collective-permute-start.5) | collective-permute-done | bytes 6176 | tf_op jit(solution)/shard_map/ppermute | solution.py:289
  24.2 2.0 %collective-permute-done.4.refs_2_ = f32[12,128]{1,0:T(8,128)S(1)} collective-permute-done((f32[12,128]{1,0:T(8,128)S(1)}, f32[12,128]{1,0:T(8,128)S(1)}, u32[]{:S(2)}, u32[]{:S(2)}) %collective-permute-start.4) | collective-permute-done | bytes 6176 | tf_op jit(solution)/shard_map/ppermute | solution.py:289
  26.2 0.0 collective-permute-done.3.refs_1_
  26.2 0.1 shard_map.117.refs_0_
  26.3 0.0 collective-permute-start.8
  26.3 1.0 %collective-permute-start.7 = (f32[7,128]{1,0:T(8,128)S(1)}, f32[7,128]{1,0:T(8,128)S(1)}, u32[]{:S(2)}, u32[]{:S(2)}) collective-permute-start(f32[7,128]{1,0:T(8,128)S(1)} %shard_map.117.refs_0_), channel_id=1, source_target_pairs={{0,2},{1,3},{2,0},{3,1},{4,6},{5,7},{6,4},{7,5},{8,10},{9,11},{10,... | collective-permute-start | bytes 10760 | tf_op jit(solution)/shard_map/ppermute | solution.py:289
  27.4 0.8 %collective-permute-start.6 = (f32[7,128]{1,0:T(8,128)S(1)}, f32[7,128]{1,0:T(8,128)S(1)}, u32[]{:S(2)}, u32[]{:S(2)}) collective-permute-start(f32[7,128]{1,0:T(8,128)S(1)} %shard_map.117.refs_0_), channel_id=1, source_target_pairs={{0,1},{1,0},{2,3},{3,2},{4,5},{5,4},{6,7},{7,6},{8,9},{9,8},{10,11... | collective-permute-start | bytes 10760 | tf_op jit(solution)/shard_map/ppermute | solution.py:289
  28.2 1.2 %collective-permute-done.8.refs_3_ = f32[7,128]{1,0:T(8,128)S(1)} collective-permute-done((f32[7,128]{1,0:T(8,128)S(1)}, f32[7,128]{1,0:T(8,128)S(1)}, u32[]{:S(2)}, u32[]{:S(2)}) %collective-permute-start.8) | collective-permute-done | bytes 3616 | tf_op jit(solution)/shard_map/ppermute | solution.py:289
  29.4 0.7 %collective-permute-done.7.refs_2_ = f32[7,128]{1,0:T(8,128)S(1)} collective-permute-done((f32[7,128]{1,0:T(8,128)S(1)}, f32[7,128]{1,0:T(8,128)S(1)}, u32[]{:S(2)}, u32[]{:S(2)}) %collective-permute-start.7) | collective-permute-done | bytes 3616 | tf_op jit(solution)/shard_map/ppermute | solution.py:289
  30.0 0.0 collective-permute-done.6.refs_1_
  30.0 0.6 %shard_map.118 = (f32[3,1,128]{2,1,0:T(1,128)}, f32[1,128]{1,0:T(1,128)}, f32[1,1]{1,0:T(1,128)}) custom-call(f32[7,128]{1,0:T(8,128)S(1)} %shard_map.117.refs_0_, f32[7,128]{1,0:T(8,128)S(1)} %collective-permute-done.6.refs_1_, f32[7,128]{1,0:T(8,128)S(1)} %collective-permute-done.7.refs_2_, f32[7,128]{1,0:T(8,128)S(1)} %collective-permute-done.8.refs_3_, ...), custom_call_target="tpu_custom_call" | custom-call | tf_op jit(solution)/shard_map/pallas_call | solution.py:393
  (3 shorter events, 0.0 us)
Async XLA Ops:
  0.6 0.7 %copy-start.7 = (f32[1,128,2]{1,2,0:T(2,128)S(1)}, f32[1,128,2]{1,2,0:T(2,128)}, u32[]{:S(2)}) copy-start(f32[1,128,2]{1,2,0:T(2,128)} %param.12) | copy-start | bytes 3076
  0.6 0.8 %copy-start.2 = (bf16[1,128,128]{2,1,0:T(8,128)(2,1)S(1)}, bf16[1,128,128]{2,1,0:T(8,128)(2,1)}, u32[]{:S(2)}) copy-start(bf16[1,128,128]{2,1,0:T(8,128)(2,1)} %param.11) | copy-start | bytes 98308
  0.7 0.8 %copy-start.3 = (s32[1,128,2,16]{1,3,2,0:T(8,128)S(1)}, s32[1,128,2,16]{1,3,2,0:T(8,128)}, u32[]{:S(2)}) copy-start(s32[1,128,2,16]{1,3,2,0:T(8,128)} %param.10) | copy-start | bytes 49156
  0.7 0.8 %copy-start.6 = (s32[1,128,2]{1,2,0:T(2,128)S(1)}, s32[1,128,2]{1,2,0:T(2,128)}, u32[]{:S(2)}) copy-start(s32[1,128,2]{1,2,0:T(2,128)} %param.9) | copy-start | bytes 3076
  1.4 5.8 %copy-start = (bf16[3,512,512]{2,1,0:T(8,128)(2,1)S(1)}, bf16[3,512,512]{2,1,0:T(8,128)(2,1)}, u32[]{:S(2)}) copy-start(bf16[3,512,512]{2,1,0:T(8,128)(2,1)} %w_hid.1) | copy-start | bytes 4718596
  1.4 5.8 %copy-start.1 = (bf16[3,144,512]{2,1,0:T(8,128)(2,1)S(1)}, bf16[3,144,512]{2,1,0:T(8,128)(2,1)}, u32[]{:S(2)}) copy-start(bf16[3,144,512]{2,1,0:T(8,128)(2,1)} %w_in.1) | copy-start | bytes 1327108
  1.5 5.8 %copy-start.4 = (bf16[3,4,512]{2,1,0:T(4,128)(2,1)S(1)}, bf16[3,4,512]{2,1,0:T(4,128)(2,1)}, u32[]{:S(2)}) copy-start(bf16[3,4,512]{2,1,0:T(4,128)(2,1)} %w_out.1) | copy-start | bytes 36868
  1.5 7.2 %collective-permute-start.2 = (bf16[176,128]{1,0:T(8,128)(2,1)S(1)}, bf16[176,128]{1,0:T(8,128)(2,1)S(1)}, u32[]{:S(2)}, u32[]{:S(2)}) collective-permute-start(bf16[176,128]{1,0:T(8,128)(2,1)S(1)} %shard_map.113.refs_0_), channel_id=1, source_target_pairs={{0,12},{4,8},{8,4},{12,0},{1,13},{5,9},{9,5},{13,1},{2,14},{6,10},... | collective-permute-start | bytes 135176 | tf_op jit(solution)/shard_map/ppermute | solution.py:289
  6.6 4.9 %collective-permute-start.1 = (bf16[176,128]{1,0:T(8,128)(2,1)S(1)}, bf16[176,128]{1,0:T(8,128)(2,1)S(1)}, u32[]{:S(2)}, u32[]{:S(2)}) collective-permute-start(bf16[176,128]{1,0:T(8,128)(2,1)S(1)} %shard_map.113.refs_0_), channel_id=1, source_target_pairs={{0,8},{4,12},{8,0},{12,4},{1,9},{5,13},{9,1},{13,5},{2,10},{6,14},... | collective-permute-start | bytes 135176 | tf_op jit(solution)/shard_map/ppermute | solution.py:289
  6.6 4.9 %collective-permute-start = (bf16[176,128]{1,0:T(8,128)(2,1)S(1)}, bf16[176,128]{1,0:T(8,128)(2,1)S(1)}, u32[]{:S(2)}, u32[]{:S(2)}) collective-permute-start(bf16[176,128]{1,0:T(8,128)(2,1)S(1)} %shard_map.113.refs_0_), channel_id=1, source_target_pairs={{0,4},{4,0},{8,12},{12,8},{1,5},{5,1},{9,13},{13,9},{2,6},{6,2},{1... | collective-permute-start | bytes 135176 | tf_op jit(solution)/shard_map/ppermute | solution.py:289
  7.3 4.3 %copy-start.5 = (f32[3,1,128]{2,1,0:T(1,128)S(1)}, f32[3,1,128]{2,1,0:T(1,128)}, u32[]{:S(2)}) copy-start(f32[3,1,128]{2,1,0:T(1,128)} %refs_4_.3) | copy-start | bytes 4612
  7.3 4.2 %copy-start.8 = (bf16[256,256]{1,0:T(8,128)(2,1)S(1)}, bf16[256,256]{1,0:T(8,128)(2,1)}, u32[]{:S(2)}) copy-start(bf16[256,256]{1,0:T(8,128)(2,1)} %constant.2.clone.refs_8_) | copy-start | bytes 393220
  18.7 5.5 %collective-permute-start.5 = (f32[12,128]{1,0:T(8,128)S(1)}, f32[12,128]{1,0:T(8,128)S(1)}, u32[]{:S(2)}, u32[]{:S(2)}) collective-permute-start(f32[12,128]{1,0:T(8,128)S(1)} %shard_map.116.refs_0_), channel_id=1, source_target_pairs={{0,12},{4,8},{8,4},{12,0},{1,13},{5,9},{9,5},{13,1},{2,14},{6,10},... | collective-permute-start | bytes 18440 | tf_op jit(solution)/shard_map/ppermute | solution.py:289
  21.7 4.5 %collective-permute-start.4 = (f32[12,128]{1,0:T(8,128)S(1)}, f32[12,128]{1,0:T(8,128)S(1)}, u32[]{:S(2)}, u32[]{:S(2)}) collective-permute-start(f32[12,128]{1,0:T(8,128)S(1)} %shard_map.116.refs_0_), channel_id=1, source_target_pairs={{0,8},{4,12},{8,0},{12,4},{1,9},{5,13},{9,1},{13,5},{2,10},{6,14},... | collective-permute-start | bytes 18440 | tf_op jit(solution)/shard_map/ppermute | solution.py:289
  21.7 4.5 %collective-permute-start.3 = (f32[12,128]{1,0:T(8,128)S(1)}, f32[12,128]{1,0:T(8,128)S(1)}, u32[]{:S(2)}, u32[]{:S(2)}) collective-permute-start(f32[12,128]{1,0:T(8,128)S(1)} %shard_map.116.refs_0_), channel_id=1, source_target_pairs={{0,4},{4,0},{8,12},{12,8},{1,5},{5,1},{9,13},{13,9},{2,6},{6,2},{1... | collective-permute-start | bytes 18440 | tf_op jit(solution)/shard_map/ppermute | solution.py:289
  26.3 3.0 %collective-permute-start.8 = (f32[7,128]{1,0:T(8,128)S(1)}, f32[7,128]{1,0:T(8,128)S(1)}, u32[]{:S(2)}, u32[]{:S(2)}) collective-permute-start(f32[7,128]{1,0:T(8,128)S(1)} %shard_map.117.refs_0_), channel_id=1, source_target_pairs={{0,3},{1,2},{2,1},{3,0},{4,7},{5,6},{6,5},{7,4},{8,11},{9,10},{10,... | collective-permute-start | bytes 10760 | tf_op jit(solution)/shard_map/ppermute | solution.py:289
  26.3 3.7 %collective-permute-start.7 = (f32[7,128]{1,0:T(8,128)S(1)}, f32[7,128]{1,0:T(8,128)S(1)}, u32[]{:S(2)}, u32[]{:S(2)}) collective-permute-start(f32[7,128]{1,0:T(8,128)S(1)} %shard_map.117.refs_0_), channel_id=1, source_target_pairs={{0,2},{1,3},{2,0},{3,1},{4,6},{5,7},{6,4},{7,5},{8,10},{9,11},{10,... | collective-permute-start | bytes 10760 | tf_op jit(solution)/shard_map/ppermute | solution.py:289
  27.4 2.7 %collective-permute-start.6 = (f32[7,128]{1,0:T(8,128)S(1)}, f32[7,128]{1,0:T(8,128)S(1)}, u32[]{:S(2)}, u32[]{:S(2)}) collective-permute-start(f32[7,128]{1,0:T(8,128)S(1)} %shard_map.117.refs_0_), channel_id=1, source_target_pairs={{0,1},{1,0},{2,3},{3,2},{4,5},{5,4},{6,7},{7,6},{8,9},{9,8},{10,11... | collective-permute-start | bytes 10760 | tf_op jit(solution)/shard_map/ppermute | solution.py:289

commit v4 on v3

--- a/solution.py
+++ b/solution.py
@@ -14,6 +14,8 @@
 DC = 16
 NBINS = 256
 EXTRA = 16
+LISTS = 64
+SPLIT = True
 
 OPPONENT = ((0.2126, 0.7152, 0.0722), (0.5, -0.5, 0.0), (0.0, 0.4, -0.4))
 SPREAD = (0.6, 0.35, 0.35)
@@ -51,14 +53,12 @@
     rows[...] = jnp.zeros_like(rows)
 
 
-def pack_kernel(visible, bins, ray_code, blend, blank, message):
+def pack_kernel(bins, ray_code, blank, message):
     pixels = ray_code.shape[0]
     listed = bins.shape[0] * bins.shape[1]
     message[0:pixels] = ray_code[...]
     message[pixels : pixels + listed] = bins[...].astype(F32).reshape(listed, pixels).astype(BF16)
-    shares = blend[...] / jnp.sum(blend[...], axis=0, keepdims=True)
-    rows = [visible[...].astype(F32)] + parts_of(shares) + [blank[...]]
-    message[pixels + listed :] = jnp.concatenate(rows, axis=0).astype(BF16)
+    message[pixels + listed :] = blank[...]
 
 
 def tiles_for(most, sizes):
@@ -66,10 +66,17 @@
     return [(high, low, high) for low, high in zip(bounds, bounds[1:])]
 
 
-def layout_kernel(samples, before, spread):
+def layout_kernel(samples, visible, blend, lines, message, before, spread):
     before[...] = (iota(before.shape, 0) < iota(before.shape, 1)).astype(F32).astype(BF16)
-    here = iota(spread.shape, 0) % samples == iota(spread.shape, 1) // DC
-    spread[...] = here.astype(F32).astype(BF16)
+    row = iota(spread.shape[1:], 0)
+    here = row % samples == iota(spread.shape[1:], 1) // DC
+    for k in range(spread.shape[0]):
+        mine = here & (row % LISTS // samples == k)
+        spread[k] = mine.astype(F32).astype(BF16)
+    shares = blend[...] / jnp.sum(blend[...], axis=0, keepdims=True)
+    rows = [visible[...].astype(F32)] + parts_of(shares)
+    rows.append(jnp.zeros((EXTRA - 4 * visible.shape[0], visible.shape[1]), F32))
+    message[message.shape[0] - EXTRA :] = jnp.concatenate(rows, axis=0).astype(BF16)
 
 
 def prepare_kernel(samples, w_in, w_hid, w_out, first_w, hid_w, last_w, sem):
@@ -92,9 +99,9 @@
     load.wait()
 
 
-def serve_kernel(sources, slots, tiles, *refs):
+def serve_kernel(own, sources, slots, tiles, *refs):
     messages = refs[:sources]
-    truth, first_w, w_hid, last_w, table, before, spread, partial = refs[sources : sources + 8]
+    aside, first_w, w_hid, last_w, table, before, spread, partial = refs[sources : sources + 8]
     places, mixed, codes, depths, heads = refs[sources + 8 :]
     local_blocks = w_hid.shape[0]
     pixels = messages[0].shape[1]
@@ -106,50 +113,61 @@
 
     named = []
     for s in range(sources):
-        for v in range(2):
-            block = iota((8, pixels), 0) + first_block
-            hit = (extras[s][v : v + 1] == block.astype(F32)) & (
-                iota((8, pixels), 0) < local_blocks
-            )
-            named.append(hit.astype(F32))
-    either = [named[2 * s] + named[2 * s + 1] for s in range(sources)]
+        block = iota((8, pixels), 0)
+        known = (block + first_block).astype(F32)
+        named.append(
+            [
+                ((extras[s][v : v + 1] == known) & (block < local_blocks)).astype(F32)
+                for v in range(2)
+            ]
+        )
+    either = [first + second for first, second in named]
     ranks = jnp.dot(
         jnp.concatenate(either, axis=0).astype(BF16), before[...], preferred_element_type=F32
     )
     offset = jnp.zeros((8, 1), F32)
     slot_row = iota((slots, pixels), 0).astype(F32)
     for s in range(sources):
-        rank = ranks[8 * s : 8 * s + 8] + offset
+        spot = jnp.where(either[s] > 0.0, ranks[8 * s : 8 * s + 8] + offset, -1.0)
         offset = offset + jnp.sum(either[s], axis=1, keepdims=True)
-        for v in range(2):
-            spot = jnp.where(named[2 * s + v] > 0.0, rank, -1.0)
-            lanes = pl.ds((2 * s + v) * pixels, pixels)
+        for k in range(local_blocks):
+            places[k * slots : (k + 1) * slots, s * pixels : (s + 1) * pixels] = (
+                (slot_row == spot[k : k + 1]).astype(F32).astype(BF16)
+            )
+    counts = [jnp.max(offset[k : k + 1]).astype(jnp.int32) for k in range(local_blocks)]
+
+    lane = iota((pixels, pixels), 1)
+    per_turn = pixels // LISTS
+    for turn in range(0, sources, per_turn):
+        group = []
+        for s in range(turn, min(turn + per_turn, sources)):
+            bins = messages[s][pixels : pixels + lists].astype(F32)
             for k in range(local_blocks):
-                places[k * slots : (k + 1) * slots, lanes] = (
-                    (slot_row == spot[k : k + 1]).astype(F32).astype(BF16)
+                group.append(
+                    jnp.where(named[s][0][k : k + 1] > 0.0, bins[:samples], bins[samples:])
                 )
-    counts = [jnp.max(offset[k : k + 1]).astype(jnp.int32) for k in range(local_blocks)]
-
-    lane = iota((pixels, pixels), 1)
-    per_turn = pixels // lists
-    for turn in range(0, sources, per_turn):
-        group = [
-            messages[s][pixels : pixels + lists].astype(F32)
-            for s in range(turn, min(turn + per_turn, sources))
-        ]
-        if len(group) < per_turn:
-            group.append(jnp.zeros(((per_turn - len(group)) * lists, pixels), F32))
+            group.append(jnp.zeros((LISTS - local_blocks * samples, pixels), F32))
+        rows = sum(part.shape[0] for part in group)
+        if rows < pixels:
+            group.append(jnp.zeros((pixels - rows, pixels), F32))
         turned = jnp.concatenate(group, axis=0).T
         for s in range(turn, min(turn + per_turn, sources)):
-            for v in range(2):
-                rows = pl.ds((2 * s + v) * pixels, pixels)
-                mine = lane // samples == 2 * (s - turn) + v
-                mixed[rows, 0:RC] = messages[s][0:pixels]
-                mixed[rows, RC:] = jnp.where(mine, turned, 0.0).astype(BF16)
+            mixed[s * pixels : (s + 1) * pixels, 0:RC] = messages[s][0:pixels]
+            mixed[s * pixels : (s + 1) * pixels, RC:] = jnp.where(
+                lane // LISTS == s - turn, turned, 0.0
+            ).astype(BF16)
 
     chosen = jnp.dot(places[...], mixed[...], preferred_element_type=F32).astype(BF16)
     codes[...] = chosen[:, :RC]
-    bins = jnp.dot(chosen[:, RC:], spread[...], preferred_element_type=F32)
+    bins = jnp.concatenate(
+        [
+            jnp.dot(
+                chosen[k * slots : (k + 1) * slots, RC:], spread[k], preferred_element_type=F32
+            )
+            for k in range(local_blocks)
+        ],
+        axis=0,
+    )
     is_bin = (bins == iota(bins.shape, 1).astype(F32)).astype(F32).astype(BF16)
     depths[...] = jnp.dot(is_bin, table[...], preferred_element_type=F32).astype(BF16)
 
@@ -209,17 +227,27 @@
     shades.append(jnp.zeros_like(background))
     shades = jnp.concatenate(shades, axis=0)[:, : local_blocks * slots]
     stacked = jnp.concatenate(parts_of(shades) + [jnp.zeros_like(shades)], axis=0).astype(BF16)
-    spots = jnp.dot(stacked, places[...], preferred_element_type=F32)
-    spots = spots[0:4] + spots[4:8] + spots[8:12]
-    sums = []
-    for s in range(sources):
-        mine = []
-        for v in range(2):
-            share = extras[s][2 + v : 3 + v] + extras[s][4 + v : 5 + v] + extras[s][6 + v : 7 + v]
-            mine.append(spots[0:3, (2 * s + v) * pixels : (2 * s + v + 1) * pixels] * share)
-        sums.append(mine[0] + mine[1])
-    sums[0] = sums[0] - truth[...].reshape(3, pixels)
-    partial[...] = jnp.concatenate(sums, axis=0)
+    sums = [jnp.zeros((3, pixels), F32)] * sources
+    for k in range(local_blocks):
+        spots = jnp.dot(
+            stacked[:, k * slots : (k + 1) * slots],
+            places[k * slots : (k + 1) * slots],
+            preferred_element_type=F32,
+        )
+        spots = spots[0:4] + spots[4:8] + spots[8:12]
+        for s in range(sources):
+            share = jnp.zeros((1, pixels), F32)
+            for v in range(2):
+                part = extras[s][2 + v : 3 + v] + extras[s][4 + v : 5 + v] + extras[s][6 + v : 7 + v]
+                share = share + named[s][v][k : k + 1] * part
+            sums[s] = sums[s] + spots[0:3, s * pixels : (s + 1) * pixels] * share
+    if own is None:
+        sums[0] = sums[0] - aside[...].reshape(3, pixels)
+        partial[...] = jnp.concatenate(sums, axis=0)
+    elif own:
+        partial[...] = sums[0] - aside[...].reshape(3, pixels)
+    else:
+        partial[...] = jnp.concatenate([aside[...]] + sums, axis=0)
 
 
 def gather_kernel(sources, *refs):
@@ -291,7 +319,7 @@
 
 
 def call(
-    kernel, out_shape, in_specs, scratch, flops=0, bytes_accessed=0, limit=8 << 20
+    kernel, out_shape, in_specs, scratch, flops=0, bytes_accessed=0, limit=8 << 20, aliases=None
 ):
     cost = None
     if flops:
@@ -302,6 +330,7 @@
         in_specs=in_specs,
         scratch_shapes=list(scratch),
         cost_estimate=cost,
+        input_output_aliases=aliases or {},
         compiler_params=pltpu.CompilerParams(vmem_limit_bytes=limit),
     )
 
@@ -321,39 +350,35 @@
     near = pl.BlockSpec(memory_space=pltpu.VMEM)
     blank = call(
         blank_kernel,
-        jax.ShapeDtypeStruct((EXTRA - 4 * visible_num, pixels), F32),
+        jax.ShapeDtypeStruct((EXTRA, pixels), BF16),
         [],
         (),
         flops=1 << 32,
         bytes_accessed=1 << 17,
     )()
-    message = call(
-        pack_kernel, jax.ShapeDtypeStruct((height, pixels), BF16), [near] * 5, ()
+    lines = call(
+        pack_kernel, jax.ShapeDtypeStruct((height, pixels), BF16), [near] * 3, ()
     )(
-        visible.reshape(pixels, visible_num).T,
         jnp.transpose(bins.reshape(pixels, visible_num, samples), (1, 2, 0)),
         ray_code.reshape(pixels, RC),
-        blend.reshape(pixels, visible_num).T,
         blank,
     )
+    message, before, spread = call(
+        functools.partial(layout_kernel, samples),
+        (
+            jax.ShapeDtypeStruct((height, pixels), BF16),
+            jax.ShapeDtypeStruct((pixels, pixels), BF16),
+            jax.ShapeDtypeStruct((local_blocks, pixels, samples * DC), BF16),
+        ),
+        [near] * 3,
+        (),
+        flops=1 << 32,
+        bytes_accessed=1 << 17,
+        aliases={2: 0},
+    )(visible.reshape(pixels, visible_num).T, blend.reshape(pixels, visible_num).T, lines)
     messages = exchange(message, "block", sources)
     table = jnp.asarray(depth_table(samples))
 
-    slots = -(-sources * capacity // 16) * 16
-    tiles = tiles_for(slots, list(range(16, slots, 16)))
-    slots_all = local_blocks * slots
-    before, spread = call(
-        functools.partial(layout_kernel, samples),
-        (
-            jax.ShapeDtypeStruct((pixels, pixels), BF16),
-            jax.ShapeDtypeStruct((pixels, samples * DC), BF16),
-        ),
-        [],
-        (),
-        limit=8 * 1024 * 1024,
-        flops=1 << 32,
-        bytes_accessed=1 << 17,
-    )()
     first_w, hid_w, last_w = call(
         functools.partial(prepare_kernel, samples),
         (
@@ -367,21 +392,33 @@
         flops=1 << 20,
         bytes_accessed=1 << 22,
     )(w_in, w_hid, w_out)
-    partial = call(
-        functools.partial(serve_kernel, sources, slots, tiles),
-        jax.ShapeDtypeStruct((3 * sources, pixels), F32),
-        [near] * (sources + 7),
-        (
-            pltpu.VMEM((slots_all, sources * visible_num * pixels), BF16),
-            pltpu.VMEM((sources * visible_num * pixels, 2 * RC), BF16),
-            pltpu.VMEM((slots_all, RC), BF16),
-            pltpu.VMEM((slots_all, samples * DC), BF16),
-            pltpu.VMEM((-(-slots_all // 128) * 128, 128), F32),
-        ),
-        flops=2 * slots_all * samples * hidden * (in_width + hidden + 4),
-        bytes_accessed=2 * (w_in.size + w_hid.size),
-        limit=40 * 1024 * 1024,
-    )(*messages, truth, first_w, hid_w, last_w, table, before, spread)
+
+    def serve(own, parts, aside):
+        count = len(parts)
+        slots = -(-count * capacity // 16) * 16
+        slots_all = local_blocks * slots
+        return call(
+            functools.partial(
+                serve_kernel, own, count, slots, tiles_for(slots, list(range(16, slots, 16)))
+            ),
+            jax.ShapeDtypeStruct((3 * count + 3 * (own is False), pixels), F32),
+            [near] * (count + 7),
+            (
+                pltpu.VMEM((slots_all, count * pixels), BF16),
+                pltpu.VMEM((count * pixels, 2 * RC), BF16),
+                pltpu.VMEM((slots_all, RC), BF16),
+                pltpu.VMEM((slots_all, samples * DC), BF16),
+                pltpu.VMEM((-(-slots_all // 128) * 128, 128), F32),
+            ),
+            flops=2 * slots_all * samples * hidden * (in_width + hidden + 4),
+            bytes_accessed=2 * (w_in.size + w_hid.size),
+            limit=40 * 1024 * 1024,
+        )(*parts, aside, first_w, hid_w, last_w, table, before, spread)
+
+    if SPLIT:
+        partial = serve(False, messages[1:], serve(True, messages[:1], truth))
+    else:
+        partial = serve(None, messages, truth)
     partials = exchange(partial, "block", sources)
     edge = call(
         functools.partial(gather_kernel, sources),

time: 30.9 us -> 30.4 us (0.984); the launches traced: 30.7 us -> 30.7 us
  Pallas kernels: 8.21 us -> 11.6 us
  waiting for transfers between devices: 8.86 us -> 5.56 us
    pallas_call x3 -> x4, Pallas kernels: 7.17 us -> 10.5 us  [the longest x2 10.5 us: serve(): call(functools.partial(serve_kernel, own, count, slots, tiles_for(slots,...]
    ppermute x9, waiting for transfers between devices: 8.86 us -> 5.56 us  [exchange(): out.append(lax.ppermute(value, axes, [(i, i ^ s) for i in range(size)]))]
  transfers between devices with their start and end apart: 9 -> 9, of which waited for: 6 -> 5; matrix products, arithmetic and copies ran while one was open for 0% -> 0% of each run, Pallas kernels for 1% -> 13%
where the time goes in v4:
time: 30.4 us; the launch traced here: 30.7 us
  starting transfers between devices  12.1 us (40%)
  Pallas kernels  11.6 us (38%)
  waiting for transfers between devices  5.56 us (18%)
  between operations  0.78 us (3%)
  local copies, waits for them, and re-layouts  0.76 us (2%)
    ppermute x9, starting transfers between devices, exchange(): out.append(lax.ppermute(value, axes, [(i, i ^ s) for i in range(size)]))  12.1 us
    pallas_call x2, Pallas kernels, serve(): call(functools.partial(serve_kernel, own, count, slots, tiles_for(slots,...  10.5 us
    ppermute x9, waiting for transfers between devices, exchange(): out.append(lax.ppermute(value, axes, [(i, i ^ s) for i in range(size)]))  5.56 us
    unnamed x18, local copies, waits for them, and re-layouts  0.76 us
    pallas_call x1, Pallas kernels, body(): call(functools.partial(finish_kernel, columns, 3 * sources * columns * pi...  0.62 us
  transfers between devices with their start and end apart: 9, of which 5 were waited for; matrix products, arithmetic and copies ran while one was open for 0% of the time, Pallas kernels for 13%

profile of v4, /device:TPU:0, one launch (start us, length us, event | category | flops | bytes accessed | tf_op | source)
XLA Modules:
  0.0 30.7 jit_solution(16865139796240613525)
XLA Ops:
  0.6 0.0 copy-start.2
  0.6 0.0 copy-start.3
  0.7 0.0 copy-start.7
  0.7 0.0 copy-start.6
  0.7 0.7 %copy-done.2 = bf16[1,128,128]{2,1,0:T(8,128)(2,1)S(1)} copy-done((bf16[1,128,128]{2,1,0:T(8,128)(2,1)S(1)}, bf16[1,128,128]{2,1,0:T(8,128)(2,1)}, u32[]{:S(2)}) %copy-start.2) | copy-done | bytes 32792
  1.4 0.0 copy-done.3
  1.4 0.0 copy-done.7
  1.4 0.0 copy-done.6
  1.4 0.0 copy-start
  1.4 0.0 copy-start.1
  1.4 0.0 copy-start.4
  1.5 0.0 copy-start.5
  1.5 0.0 copy-start.8
  1.5 5.1 %collective-permute-start.2 = (bf16[176,128]{1,0:T(8,128)(2,1)S(1)}, bf16[176,128]{1,0:T(8,128)(2,1)S(1)}, u32[]{:S(2)}, u32[]{:S(2)}) collective-permute-start(bf16[176,128]{1,0:T(8,128)(2,1)S(1)} %get-tuple-element.12.refs_0_), channel_id=1, source_target_pairs={{0,12},{4,8},{8,4},{12,0},{1,13},{5,9},{9,5},{13,1},{2,14},{6,10},... | collective-permute-start | bytes 135176 | tf_op jit(solution)/shard_map/ppermute | solution.py:317
  6.6 0.0 collective-permute-start.1
  6.6 0.6 %collective-permute-start = (bf16[176,128]{1,0:T(8,128)(2,1)S(1)}, bf16[176,128]{1,0:T(8,128)(2,1)S(1)}, u32[]{:S(2)}, u32[]{:S(2)}) collective-permute-start(bf16[176,128]{1,0:T(8,128)(2,1)S(1)} %get-tuple-element.12.refs_0_), channel_id=1, source_target_pairs={{0,4},{4,0},{8,12},{12,8},{1,5},{5,1},{9,13},{13,9},{2,6},{6,2},{1... | collective-permute-start | bytes 135176 | tf_op jit(solution)/shard_map/ppermute | solution.py:317
  7.3 0.0 copy-done
  7.3 0.0 copy-done.1
  7.3 0.0 copy-done.4
  7.3 0.3 shard_map.115
  7.6 0.0 copy-done.5
  7.6 0.0 copy-done.8
  7.6 3.8 %shard_map.116.refs_3_ = f32[3,128]{1,0:T(4,128)S(1)} custom-call(bf16[176,128]{1,0:T(8,128)(2,1)S(1)} %get-tuple-element.12.refs_0_, f32[3,1,128]{2,1,0:T(1,128)S(1)} %copy-done.5, bf16[3,256,512]{2,1,0:T(8,128)(2,1)S(1)} %get-tuple-element.13.refs_2_.refs_4_, bf16[3,512,512]{2,1,0:T(8,128)(2,1)S(1)} %get-tuple-element.14.refs_3_.refs_5_, ...), custom_call_target="tpu_custom_call" | custom-call | flops 1557135360 | bytes 2015232 | tf_op jit(solution)/shard_map/pallas_call | solution.py:400
  11.4 0.0 collective-permute-done.2.refs_2_
  11.4 0.2 collective-permute-done.1.refs_1_
  11.6 0.0 collective-permute-done.refs_0_
  11.6 6.7 %shard_map.117.refs_0_ = f32[12,128]{1,0:T(8,128)S(1)} custom-call(bf16[176,128]{1,0:T(8,128)(2,1)S(1)} %collective-permute-done.refs_0_, bf16[176,128]{1,0:T(8,128)(2,1)S(1)} %collective-permute-done.1.refs_1_, bf16[176,128]{1,0:T(8,128)(2,1)S(1)} %collective-permute-done.2.refs_2_, f32[3,128]{1,0:T(4,128)S(1)} %shard_map.116.refs_3_, ...), custom_call_target="tpu_custom_call" | custom-call | flops 4671406080 | bytes 2015232 | tf_op jit(solution)/shard_map/pallas_call | solution.py:400
  18.3 3.4 %collective-permute-start.5 = (f32[12,128]{1,0:T(8,128)S(1)}, f32[12,128]{1,0:T(8,128)S(1)}, u32[]{:S(2)}, u32[]{:S(2)}) collective-permute-start(f32[12,128]{1,0:T(8,128)S(1)} %shard_map.117.refs_0_), channel_id=1, source_target_pairs={{0,12},{4,8},{8,4},{12,0},{1,13},{5,9},{9,5},{13,1},{2,14},{6,10},... | collective-permute-start | bytes 18440 | tf_op jit(solution)/shard_map/ppermute | solution.py:317
  21.8 0.0 collective-permute-start.4
  21.8 1.0 %collective-permute-start.3 = (f32[12,128]{1,0:T(8,128)S(1)}, f32[12,128]{1,0:T(8,128)S(1)}, u32[]{:S(2)}, u32[]{:S(2)}) collective-permute-start(f32[12,128]{1,0:T(8,128)S(1)} %shard_map.117.refs_0_), channel_id=1, source_target_pairs={{0,4},{4,0},{8,12},{12,8},{1,5},{5,1},{9,13},{13,9},{2,6},{6,2},{1... | collective-permute-start | bytes 18440 | tf_op jit(solution)/shard_map/ppermute | solution.py:317
  22.8 1.1 %collective-permute-done.5.refs_3_ = f32[12,128]{1,0:T(8,128)S(1)} collective-permute-done((f32[12,128]{1,0:T(8,128)S(1)}, f32[12,128]{1,0:T(8,128)S(1)}, u32[]{:S(2)}, u32[]{:S(2)}) %collective-permute-start.5) | collective-permute-done | bytes 6176 | tf_op jit(solution)/shard_map/ppermute | solution.py:317
  23.9 2.5 %collective-permute-done.4.refs_2_ = f32[12,128]{1,0:T(8,128)S(1)} collective-permute-done((f32[12,128]{1,0:T(8,128)S(1)}, f32[12,128]{1,0:T(8,128)S(1)}, u32[]{:S(2)}, u32[]{:S(2)}) %collective-permute-start.4) | collective-permute-done | bytes 6176 | tf_op jit(solution)/shard_map/ppermute | solution.py:317
  26.3 0.0 collective-permute-done.3.refs_1_
  26.3 0.1 shard_map.118.refs_0_
  26.4 0.0 collective-permute-start.8
  26.4 1.2 %collective-permute-start.7 = (f32[7,128]{1,0:T(8,128)S(1)}, f32[7,128]{1,0:T(8,128)S(1)}, u32[]{:S(2)}, u32[]{:S(2)}) collective-permute-start(f32[7,128]{1,0:T(8,128)S(1)} %shard_map.118.refs_0_), channel_id=1, source_target_pairs={{0,2},{1,3},{2,0},{3,1},{4,6},{5,7},{6,4},{7,5},{8,10},{9,11},{10,... | collective-permute-start | bytes 10760 | tf_op jit(solution)/shard_map/ppermute | solution.py:317
  27.7 0.6 %collective-permute-start.6 = (f32[7,128]{1,0:T(8,128)S(1)}, f32[7,128]{1,0:T(8,128)S(1)}, u32[]{:S(2)}, u32[]{:S(2)}) collective-permute-start(f32[7,128]{1,0:T(8,128)S(1)} %shard_map.118.refs_0_), channel_id=1, source_target_pairs={{0,1},{1,0},{2,3},{3,2},{4,5},{5,4},{6,7},{7,6},{8,9},{9,8},{10,11... | collective-permute-start | bytes 10760 | tf_op jit(solution)/shard_map/ppermute | solution.py:317
  28.3 1.2 %collective-permute-done.8.refs_3_ = f32[7,128]{1,0:T(8,128)S(1)} collective-permute-done((f32[7,128]{1,0:T(8,128)S(1)}, f32[7,128]{1,0:T(8,128)S(1)}, u32[]{:S(2)}, u32[]{:S(2)}) %collective-permute-start.8) | collective-permute-done | bytes 3616 | tf_op jit(solution)/shard_map/ppermute | solution.py:317
  29.5 0.7 %collective-permute-done.7.refs_2_ = f32[7,128]{1,0:T(8,128)S(1)} collective-permute-done((f32[7,128]{1,0:T(8,128)S(1)}, f32[7,128]{1,0:T(8,128)S(1)}, u32[]{:S(2)}, u32[]{:S(2)}) %collective-permute-start.7) | collective-permute-done | bytes 3616 | tf_op jit(solution)/shard_map/ppermute | solution.py:317
  30.1 0.0 collective-permute-done.6.refs_1_
  30.1 0.6 %shard_map.119 = (f32[3,1,128]{2,1,0:T(1,128)}, f32[1,128]{1,0:T(1,128)}, f32[1,1]{1,0:T(1,128)}) custom-call(f32[7,128]{1,0:T(8,128)S(1)} %shard_map.118.refs_0_, f32[7,128]{1,0:T(8,128)S(1)} %collective-permute-done.6.refs_1_, f32[7,128]{1,0:T(8,128)S(1)} %collective-permute-done.7.refs_2_, f32[7,128]{1,0:T(8,128)S(1)} %collective-permute-done.8.refs_3_, ...), custom_call_target="tpu_custom_call" | custom-call | tf_op jit(solution)/shard_map/pallas_call | solution.py:430
  (3 shorter events, 0.1 us)
Async XLA Ops:
  0.6 0.8 %copy-start.2 = (bf16[1,128,128]{2,1,0:T(8,128)(2,1)S(1)}, bf16[1,128,128]{2,1,0:T(8,128)(2,1)}, u32[]{:S(2)}) copy-start(bf16[1,128,128]{2,1,0:T(8,128)(2,1)} %param.11) | copy-start | bytes 98308
  0.6 0.8 %copy-start.3 = (s32[1,128,2,16]{1,3,2,0:T(8,128)S(1)}, s32[1,128,2,16]{1,3,2,0:T(8,128)}, u32[]{:S(2)}) copy-start(s32[1,128,2,16]{1,3,2,0:T(8,128)} %param.10) | copy-start | bytes 49156
  0.7 0.8 %copy-start.7 = (f32[1,128,2]{1,2,0:T(2,128)S(1)}, f32[1,128,2]{1,2,0:T(2,128)}, u32[]{:S(2)}) copy-start(f32[1,128,2]{1,2,0:T(2,128)} %param.12) | copy-start | bytes 3076
  0.7 0.8 %copy-start.6 = (s32[1,128,2]{1,2,0:T(2,128)S(1)}, s32[1,128,2]{1,2,0:T(2,128)}, u32[]{:S(2)}) copy-start(s32[1,128,2]{1,2,0:T(2,128)} %param.9) | copy-start | bytes 3076
  1.4 5.9 %copy-start = (bf16[3,512,512]{2,1,0:T(8,128)(2,1)S(1)}, bf16[3,512,512]{2,1,0:T(8,128)(2,1)}, u32[]{:S(2)}) copy-start(bf16[3,512,512]{2,1,0:T(8,128)(2,1)} %w_hid.1) | copy-start | bytes 4718596
  1.4 5.9 %copy-start.1 = (bf16[3,144,512]{2,1,0:T(8,128)(2,1)S(1)}, bf16[3,144,512]{2,1,0:T(8,128)(2,1)}, u32[]{:S(2)}) copy-start(bf16[3,144,512]{2,1,0:T(8,128)(2,1)} %w_in.1) | copy-start | bytes 1327108
  1.4 5.8 %copy-start.4 = (bf16[3,4,512]{2,1,0:T(4,128)(2,1)S(1)}, bf16[3,4,512]{2,1,0:T(4,128)(2,1)}, u32[]{:S(2)}) copy-start(bf16[3,4,512]{2,1,0:T(4,128)(2,1)} %w_out.1) | copy-start | bytes 36868
  1.5 6.1 %copy-start.5 = (f32[3,1,128]{2,1,0:T(1,128)S(1)}, f32[3,1,128]{2,1,0:T(1,128)}, u32[]{:S(2)}) copy-start(f32[3,1,128]{2,1,0:T(1,128)} %refs_4_.1) | copy-start | bytes 4612
  1.5 6.1 %copy-start.8 = (bf16[256,256]{1,0:T(8,128)(2,1)S(1)}, bf16[256,256]{1,0:T(8,128)(2,1)}, u32[]{:S(2)}) copy-start(bf16[256,256]{1,0:T(8,128)(2,1)} %constant.2.clone.refs_5_.refs_7_) | copy-start | bytes 393220
  1.5 9.9 %collective-permute-start.2 = (bf16[176,128]{1,0:T(8,128)(2,1)S(1)}, bf16[176,128]{1,0:T(8,128)(2,1)S(1)}, u32[]{:S(2)}, u32[]{:S(2)}) collective-permute-start(bf16[176,128]{1,0:T(8,128)(2,1)S(1)} %get-tuple-element.12.refs_0_), channel_id=1, source_target_pairs={{0,12},{4,8},{8,4},{12,0},{1,13},{5,9},{9,5},{13,1},{2,14},{6,10},... | collective-permute-start | bytes 135176 | tf_op jit(solution)/shard_map/ppermute | solution.py:317
  6.6 4.9 %collective-permute-start.1 = (bf16[176,128]{1,0:T(8,128)(2,1)S(1)}, bf16[176,128]{1,0:T(8,128)(2,1)S(1)}, u32[]{:S(2)}, u32[]{:S(2)}) collective-permute-start(bf16[176,128]{1,0:T(8,128)(2,1)S(1)} %get-tuple-element.12.refs_0_), channel_id=1, source_target_pairs={{0,8},{4,12},{8,0},{12,4},{1,9},{5,13},{9,1},{13,5},{2,10},{6,14},... | collective-permute-start | bytes 135176 | tf_op jit(solution)/shard_map/ppermute | solution.py:317
  6.6 4.9 %collective-permute-start = (bf16[176,128]{1,0:T(8,128)(2,1)S(1)}, bf16[176,128]{1,0:T(8,128)(2,1)S(1)}, u32[]{:S(2)}, u32[]{:S(2)}) collective-permute-start(bf16[176,128]{1,0:T(8,128)(2,1)S(1)} %get-tuple-element.12.refs_0_), channel_id=1, source_target_pairs={{0,4},{4,0},{8,12},{12,8},{1,5},{5,1},{9,13},{13,9},{2,6},{6,2},{1... | collective-permute-start | bytes 135176 | tf_op jit(solution)/shard_map/ppermute | solution.py:317
  18.3 5.5 %collective-permute-start.5 = (f32[12,128]{1,0:T(8,128)S(1)}, f32[12,128]{1,0:T(8,128)S(1)}, u32[]{:S(2)}, u32[]{:S(2)}) collective-permute-start(f32[12,128]{1,0:T(8,128)S(1)} %shard_map.117.refs_0_), channel_id=1, source_target_pairs={{0,12},{4,8},{8,4},{12,0},{1,13},{5,9},{9,5},{13,1},{2,14},{6,10},... | collective-permute-start | bytes 18440 | tf_op jit(solution)/shard_map/ppermute | solution.py:317
  21.8 4.5 %collective-permute-start.4 = (f32[12,128]{1,0:T(8,128)S(1)}, f32[12,128]{1,0:T(8,128)S(1)}, u32[]{:S(2)}, u32[]{:S(2)}) collective-permute-start(f32[12,128]{1,0:T(8,128)S(1)} %shard_map.117.refs_0_), channel_id=1, source_target_pairs={{0,8},{4,12},{8,0},{12,4},{1,9},{5,13},{9,1},{13,5},{2,10},{6,14},... | collective-permute-start | bytes 18440 | tf_op jit(solution)/shard_map/ppermute | solution.py:317
  21.8 4.5 %collective-permute-start.3 = (f32[12,128]{1,0:T(8,128)S(1)}, f32[12,128]{1,0:T(8,128)S(1)}, u32[]{:S(2)}, u32[]{:S(2)}) collective-permute-start(f32[12,128]{1,0:T(8,128)S(1)} %shard_map.117.refs_0_), channel_id=1, source_target_pairs={{0,4},{4,0},{8,12},{12,8},{1,5},{5,1},{9,13},{13,9},{2,6},{6,2},{1... | collective-permute-start | bytes 18440 | tf_op jit(solution)/shard_map/ppermute | solution.py:317
  26.4 3.0 %collective-permute-start.8 = (f32[7,128]{1,0:T(8,128)S(1)}, f32[7,128]{1,0:T(8,128)S(1)}, u32[]{:S(2)}, u32[]{:S(2)}) collective-permute-start(f32[7,128]{1,0:T(8,128)S(1)} %shard_map.118.refs_0_), channel_id=1, source_target_pairs={{0,3},{1,2},{2,1},{3,0},{4,7},{5,6},{6,5},{7,4},{8,11},{9,10},{10,... | collective-permute-start | bytes 10760 | tf_op jit(solution)/shard_map/ppermute | solution.py:317
  26.4 3.7 %collective-permute-start.7 = (f32[7,128]{1,0:T(8,128)S(1)}, f32[7,128]{1,0:T(8,128)S(1)}, u32[]{:S(2)}, u32[]{:S(2)}) collective-permute-start(f32[7,128]{1,0:T(8,128)S(1)} %shard_map.118.refs_0_), channel_id=1, source_target_pairs={{0,2},{1,3},{2,0},{3,1},{4,6},{5,7},{6,4},{7,5},{8,10},{9,11},{10,... | collective-permute-start | bytes 10760 | tf_op jit(solution)/shard_map/ppermute | solution.py:317
  27.7 2.4 %collective-permute-start.6 = (f32[7,128]{1,0:T(8,128)S(1)}, f32[7,128]{1,0:T(8,128)S(1)}, u32[]{:S(2)}, u32[]{:S(2)}) collective-permute-start(f32[7,128]{1,0:T(8,128)S(1)} %shard_map.118.refs_0_), channel_id=1, source_target_pairs={{0,1},{1,0},{2,3},{3,2},{4,5},{5,4},{6,7},{7,6},{8,9},{9,8},{10,11... | collective-permute-start | bytes 10760 | tf_op jit(solution)/shard_map/ppermute | solution.py:317
